TPU v7x, 128 devices: a whole 4x4x4 slice. The times are simulated.
128 devices in a mesh: dp: 16 (over y, x), mp: 8 (over z, core).
Axes of the slice: x: 4, y: 4, z: 4, core: 2. Of those that a mesh axis runs over, the one named last changes fastest.
Arguments:
- inner_before_nonlinear: bfloat16 [8192, 10240], P('dp', 'mp'), may hold values from -6 to 6
- layer_exit_derivative: bfloat16 [8192, 5120], P('dp', 'mp'), may hold values from -6 to 6
- contract_weights: bfloat16 [10240, 5120], P('mp'), may hold values from -0.0625 to 0.0625
- copy_tile_indicator: int32 [16, 8, 51200], P('dp', 'mp'), may hold values from 0 to 1, as said below
- span_opening_tile: int32 [17], replicated, may hold values from 0 to 51200, as said below
- remaining_tile_flags: int32 [8, 51200], P('mp'), may hold values from 0 to 1, as said below
Outputs:
- pre_grad: bfloat16 [8192, 10240], P('dp', 'mp')
- grad_blocks: float32 [8, 6400, 128], P('mp')
Inputs may be any that keep to these rules, and one draw needn't show every extreme that they name: `copy_tile_indicator`: in every region, at most 1600 ones of one replica and one index of mp; in every draw one region holds exactly 1600 from every replica. `span_opening_tile`: starts at 0 and ends at 51200; each region holds 1600 to 4800 blocks, and some region exactly 4800. `remaining_tile_flags`: at most 400 ones in each region of each row; some region holds exactly 400.
All inputs are finite; a program needn't handle non-finite values.
Results may differ from a plain program's by a relative error of at most 0.013.
Values may be sent and summed in bfloat16 or wider, within the bound.
A program may use at most 192 MiB of HBM per device.

v0:
```python
import math

import jax
import jax.numpy as jnp
from jax import lax
from jax.sharding import PartitionSpec as P

half_root = 0.7071067811865476
inv_root_tau = 0.3989422804014327


def gelu_parts(inner_before_nonlinear):
    values = inner_before_nonlinear.astype(jnp.float32)
    normal_cdf = 0.5 * (1.0 + jax.scipy.special.erf(values * half_root))
    density = jnp.exp(-0.5 * values * values) * inv_root_tau
    return (values * normal_cdf, normal_cdf + values * density)


def local(
    inner_before_nonlinear,
    layer_exit_derivative,
    contract_weights,
    copy_tile_indicator,
    span_opening_tile,
    remaining_tile_flags,
):
    replicas = lax.axis_size("dp")
    owner_index = lax.axis_index("dp")
    tokens_local, hidden_local = inner_before_nonlinear.shape
    width_full = contract_weights.shape[1]
    blocks_local = hidden_local * width_full // 128
    base_count = blocks_local // replicas
    widest_span_tally = base_count + base_count // 2
    keep_most = base_count // 8
    full_grad = lax.all_gather(layer_exit_derivative, "mp", axis=1, tiled=True)
    activation, gelu_slope = gelu_parts(inner_before_nonlinear)
    activation = activation.astype(jnp.bfloat16)
    grad_scale = 1.0 / math.sqrt(tokens_local * replicas)
    weight_grad = (
        lax.dot_general(
            activation, full_grad, (((0,), (0,)), ((), ())), preferred_element_type=jnp.float32
        )
        * grad_scale
    ).astype(jnp.bfloat16)
    grad_rows = weight_grad.reshape(blocks_local, 128)
    act_grad = lax.dot_general(
        full_grad, contract_weights, (((1,), (1,)), ((), ())), preferred_element_type=jnp.float32
    )
    pre_grad = (act_grad * gelu_slope).astype(jnp.bfloat16)
    selected = copy_tile_indicator[0, 0]
    masked = jnp.where((selected == 1)[:, None], grad_rows, jnp.zeros_like(grad_rows))
    extended = jnp.concatenate([masked, jnp.zeros((widest_span_tally, 128), jnp.bfloat16)], axis=0)
    starts = span_opening_tile[:replicas]
    widths = span_opening_tile[1 : replicas + 1] - starts

    def region_window(start):
        return lax.dynamic_slice_in_dim(extended, start, widest_span_tally, 0)

    windows = jax.vmap(region_window)(starts)
    inside = jnp.arange(widest_span_tally, dtype=jnp.int32)[None, :] < widths[:, None]
    dense_term = jnp.where(inside[:, :, None], windows, jnp.zeros_like(windows)).reshape(
        replicas * widest_span_tally, 128
    )
    region_sum = lax.psum_scatter(dense_term, "dp", scatter_dimension=0, tiled=True).astype(
        jnp.float32
    )
    region_low = span_opening_tile[owner_index]
    size_here = span_opening_tile[owner_index + 1] - region_low
    openings_extended = jnp.concatenate(
        [remaining_tile_flags[0], jnp.zeros((widest_span_tally,), jnp.int32)]
    )
    window = lax.dynamic_slice_in_dim(openings_extended, region_low, widest_span_tally)
    positions = jnp.arange(widest_span_tally, dtype=jnp.int32)
    is_valid = (positions < size_here) & (window == 1)
    rank_kept = jnp.cumsum(is_valid.astype(jnp.int32))
    slots = jnp.arange(keep_most, dtype=jnp.int32)
    source_row = jnp.sum((rank_kept[None, :] <= slots[:, None]).astype(jnp.int32), axis=1)
    source_row = jnp.minimum(source_row, widest_span_tally - 1)
    filled = slots < rank_kept[widest_span_tally - 1]
    picked = jnp.take(region_sum, source_row, axis=0)
    compact = jnp.where(filled[:, None], picked, jnp.zeros_like(picked))
    gathered = lax.all_gather(compact.astype(jnp.bfloat16), "dp", axis=0, tiled=True).astype(
        compact.dtype
    )
    return (pre_grad, gathered[None])


def solution(mesh):
    in_specs = (
        P("dp", "mp"),
        P("dp", "mp"),
        P("mp", None),
        P("dp", "mp", None),
        P(),
        P("mp", None),
    )
    out_specs = (P("dp", "mp"), P("mp", None, None))
    return jax.shard_map(local, mesh=mesh, in_specs=in_specs, out_specs=out_specs, check_vma=False)
```

profile of v0, /device:TPU:0, one launch (start us, length us, event | category | flops | bytes accessed | tf_op | source)
XLA Modules:
  0.0 412.6 jit_solution(2351766684422194737)
XLA Ops:
  7.2 0.7 all-gather.3.cloned.1.call-update
  8.0 0.8 slice_subtract_fusion
  9.1 1.5 compare_reduce_fusion
  10.7 38.2 %all-gather.3.cloned.1.call-done = bf16[512,5120]{1,0:T(8,128)(2,1)} async-done(((bf16[512,640]{1,0:T(8,128)(2,1)}), bf16[512,5120]{1,0:T(8,128)(2,1)}) %all-gather.3.cloned.1.call-update) | async-done | bytes 5242896 | tf_op jit(solution)/shard_map/all_gather | solution.py:35
  48.9 12.8 %multiply_convert_fusion = bf16[1280,5120]{1,0:T(8,128)(2,1)} fusion(bf16[512,5120]{1,0:T(8,128)(2,1)} %all-gather.3.cloned.1.call-done, bf16[512,1280]{1,0:T(8,128)(2,1)} %param.6), kind=kOutput, calls=%fused_computation.3 | convolution fusion | flops 6727925760 | bytes 19660800 | tf_op jit(solution)/shard_map/dot_general | solution.py:40
  61.7 19.7 %reshape.82 = bf16[51200,128]{1,0:T(8,128)(2,1)} reshape(bf16[1280,5120]{1,0:T(8,128)(2,1)} %multiply_convert_fusion) | data formatting | bytes 26214400 | tf_op jit(solution)/shard_map/reshape | solution.py:45
  81.4 27.6 %broadcast_select_fusion = bf16[51200,128]{1,0:T(8,128)(2,1)S(1)} fusion(bf16[51200,128]{1,0:T(8,128)(2,1)} %reshape.82, pred[51200]{0:T(1024)(128)(4,1)S(1)} %compare_reduce_fusion), kind=kLoop, calls=%fused_computation.5 | loop fusion | flops 6553600 | bytes 26265600 | tf_op jit(solution)/shard_map/jit(_where)/select_n | solution.py:51
  109.0 17.2 %concatenate.10 = bf16[56000,128]{1,0:T(8,128)(2,1)} pad(bf16[51200,128]{1,0:T(8,128)(2,1)S(1)} %broadcast_select_fusion, bf16[]{:T(256)} %constant.17.clone.1), padding=0_4800x0_0 | pad | bytes 27443202 | tf_op jit(solution)/shard_map/concatenate | solution.py:52
  126.2 62.5 %while.1 = (s32[]{:T(128)}, bf16[56000,128]{1,0:T(8,128)(2,1)}, s32[16,2]{0,1:T(2,128)S(1)}, bf16[16,4800,128]{2,1,0:T(8,128)(2,1)}, s32[]{:T(128)}) while((s32[]{:T(128)}, bf16[56000,128]{1,0:T(8,128)(2,1)}, s32[16,2]{0,1:T(2,128)S(1)}, bf16[16,4800,128]{2,1,0:T(8,128)(2,1)}, s32[]{:T(128)}) %tuple.23), condition=%wide.while_cond, body=%wide.while_body.sunk | while | flops 2 | bytes 2458213 | solution.py:57
  126.3 0.5 slice.48
  126.8 3.3 bitcast_dynamic-update-slice_fusion.2
  130.2 0.5 slice.48
  130.7 3.3 bitcast_dynamic-update-slice_fusion.2
  134.1 0.5 slice.48
  134.6 3.3 bitcast_dynamic-update-slice_fusion.2
  138.0 0.5 slice.48
  138.5 3.3 bitcast_dynamic-update-slice_fusion.2
  141.9 0.5 slice.48
  142.4 3.3 bitcast_dynamic-update-slice_fusion.2
  145.8 0.5 slice.48
  146.3 3.3 bitcast_dynamic-update-slice_fusion.2
  149.7 0.5 slice.48
  150.2 3.3 bitcast_dynamic-update-slice_fusion.2
  153.6 0.5 slice.48
  154.1 3.4 bitcast_dynamic-update-slice_fusion.2
  157.6 0.5 slice.48
  158.1 3.3 bitcast_dynamic-update-slice_fusion.2
  162.0 3.3 bitcast_dynamic-update-slice_fusion.2
  165.4 0.5 slice.48
  165.9 3.4 bitcast_dynamic-update-slice_fusion.2
  169.9 3.3 bitcast_dynamic-update-slice_fusion.2
  173.2 0.5 slice.48
  173.7 3.3 bitcast_dynamic-update-slice_fusion.2
  177.1 0.5 slice.48
  177.6 3.3 bitcast_dynamic-update-slice_fusion.2
  181.5 3.3 bitcast_dynamic-update-slice_fusion.2
  185.4 3.3 bitcast_dynamic-update-slice_fusion.2
  188.7 41.4 %bitcast_select_fusion = bf16[76800,128]{1,0:T(8,128)(2,1)} fusion(bf16[16,4800,128]{2,1,0:T(8,128)(2,1)} %get-tuple-element.9, pred[76800]{0:T(1024)(128)(4,1)S(1)} %lt.81), kind=kLoop, calls=%fused_computation.4 | loop fusion | flops 9830400 | bytes 39398400 | tf_op jit(solution)/shard_map/jit(_where)/select_n | solution.py:61
  230.7 0.6 fusion.13
  235.3 0.6 slice.41
  235.9 0.9 convert_reduce_fusion
  236.8 0.7 iota_compare_fusion.3
  237.5 117.8 %reduce-scatter.2.cloned.1.call-done = bf16[4800,128]{1,0:T(8,128)(2,1)} async-done(((bf16[76800,128]{1,0:T(8,128)(2,1)}), bf16[4800,128]{1,0:T(8,128)(2,1)}) %reduce-scatter.2.cloned.1.call-update) | async-done | bytes 1228816 | tf_op jit(solution)/shard_map/reduce_scatter | solution.py:64
  355.3 2.6 gather_fusion
  357.9 0.8 select_convert_fusion
  358.7 14.1 %fusion = bf16[512,1280]{1,0:T(8,128)(2,1)} fusion(bf16[512,5120]{1,0:T(8,128)(2,1)} %all-gather.3.cloned.1.call-done, bf16[1280,5120]{1,0:T(8,128)(2,1)} %param.8, bf16[512,1280]{1,0:T(8,128)(2,1)S(1)} %copy-done.2), kind=kOutput, calls=%fused_computation.14 | convolution fusion | flops 6718095360 | bytes 20971520 | tf_op jit(solution)/shard_map/dot_general | solution.py:46
  372.9 29.9 %all-gather.5.cloned.1.call-done = bf16[6400,128]{1,0:T(8,128)(2,1)} async-done(((bf16[400,128]{1,0:T(8,128)(2,1)}), bf16[6400,128]{1,0:T(8,128)(2,1)}) %all-gather.5.cloned.1.call-update) | async-done | bytes 1638416 | tf_op jit(solution)/shard_map/all_gather | solution.py:82
  402.7 3.3 bitcast_convert_fusion
  (45 shorter events, 5.0 us)
Async XLA Ops:
  7.2 41.7 %all-gather.3.cloned.1.call-start = ((), (), s32[]{:S(2)}) async-start(), calls=%async_computation.1 | async-start | bytes 5898240 | tf_op jit(solution)/shard_map/all_gather | solution.py:35
  7.9 347.4 %reduce-scatter.2.cloned.1.call-start = ((), (), s32[]{:S(2)}) async-start(), calls=%async_computation.2 | async-start | bytes 20889600 | tf_op jit(solution)/shard_map/reduce_scatter | solution.py:64
  230.1 0.7 copy-start.1
  230.1 4.5 %copy-start = (s32[1,51200]{1,0:T(1,128)S(1)}, s32[1,51200]{1,0:T(1,128)}, u32[]{:S(2)}) copy-start(s32[1,51200]{1,0:T(1,128)} %param.11) | copy-start | bytes 614404
  230.1 128.6 %copy-start.2 = (bf16[512,1280]{1,0:T(8,128)(2,1)S(1)}, bf16[512,1280]{1,0:T(8,128)(2,1)}, u32[]{:S(2)}) copy-start(bf16[512,1280]{1,0:T(8,128)(2,1)} %param.6) | copy-start | bytes 3932164
  230.1 172.6 %all-gather.5.cloned.1.call-start = ((), (), s32[]{:S(2)}) async-start(), calls=%async_computation.3 | async-start | bytes 1740800 | tf_op jit(solution)/shard_map/all_gather | solution.py:82
Sparse Core Ops, SparseCore 0:
  9.7 39.1 all-gather.2
  230.3 124.9 reduce-scatter.1
  358.9 43.8 all-gather.4
where the time goes:
time: 414 us; the launch traced here: 413 us
  waiting for transfers between devices  187 us (45%)
  local copies, waits for them, and re-layouts  104 us (25%)
  other arithmetic  77.7 us (19%)
  matrix products  26.9 us (6%)
  between operations  17.1 us (4%)
    reduce_scatter x1, waiting for transfers between devices, local(): lax.psum_scatter(dense_term, 'dp', scatter_dimension=0, tiled=True)  118 us
    gather x48, local copies, waits for them, and re-layouts  62.4 us
    select_n x1, other arithmetic, local(): jnp.where(inside[:, :, None], windows, jnp.zeros_like(windows))  41.4 us
    all_gather x1, waiting for transfers between devices, local(): full_grad = lax.all_gather(layer_exit_derivative, 'mp', axis=1, tiled=True)  38.2 us
    all_gather x1, waiting for transfers between devices, local(): lax.all_gather(compact.astype(jnp.bfloat16), 'dp', axis=0, tiled=True)  29.9 us
    select_n x1, other arithmetic, local(): jnp.where((selected == 1)[:, None], grad_rows, jnp.zeros_like(grad_rows))  27.6 us
    reshape x1, local copies, waits for them, and re-layouts, local(): grad_rows = weight_grad.reshape(blocks_local, 128)  19.7 us
    concatenate x1, local copies, waits for them, and re-layouts, local(): jnp.concatenate([masked, jnp.zeros((widest_span_tally, 128), jnp.bfloat16...  17.2 us
  transfers between devices with their start and end apart: 3, of which 3 were waited for; matrix products, arithmetic and copies ran while one was open for 5% of the time, Pallas kernels for 0%

commit v1 on v0

v1 whole, which is shorter than its diff:
```python
import functools
import math

import jax
import jax.numpy as jnp
from jax import lax
from jax.experimental import pallas as pl
from jax.experimental.pallas import tpu as pltpu
from jax.sharding import PartitionSpec as P

half_root = 0.7071067811865476
inv_root_tau = 0.3989422804014327
MESH = pl.DeviceIdType.MESH

TOK = 512
HID = 1280
WIDTH = 5120
PART = 640
PAIR = 2 * PART
LANES = 128
COLS = WIDTH // LANES
NBLK = HID * COLS
KEEP = 400
HALF = TOK // 2
GROUP = 16
SPLIT = ((0, 112, 96), (208, 96, 96))


def slot_sources(flags, copied, starts):
    rows = NBLK // LANES
    flag_rows = flags.reshape(rows, LANES)
    lane = lax.broadcasted_iota(jnp.int32, (LANES, LANES), 0)
    tri = (lane <= lane.T).astype(jnp.bfloat16)
    within = jnp.dot(flag_rows.astype(jnp.bfloat16), tri, preferred_element_type=jnp.float32)
    totals = within[:, LANES - 1]
    before = jnp.sum(
        jnp.where(jnp.arange(rows)[None, :] < jnp.arange(rows)[:, None], totals[None, :], 0.0), axis=1
    )
    upto = (before + totals).astype(jnp.int32)
    totals = totals.astype(jnp.int32)
    block = jnp.arange(NBLK, dtype=jnp.int32)
    base = jnp.sum(jnp.where(block[None, :] < starts[:, None], flags[None, :], 0), axis=1)
    slot = jnp.arange(KEEP, dtype=jnp.int32)
    target = (base[:-1, None] + slot[None, :]).reshape(-1)
    filled = (slot[None, :] < (base[1:] - base[:-1])[:, None]).reshape(-1)
    passed = upto[None, :] <= target[:, None]
    row = jnp.sum(passed.astype(jnp.int32), axis=1)
    rest = target - jnp.sum(jnp.where(passed, totals[None, :], 0), axis=1)
    pick = (row[:, None] == jnp.arange(rows)[None, :]).astype(jnp.bfloat16)
    table = jnp.concatenate(
        [within.astype(jnp.bfloat16), copied.reshape(rows, LANES).astype(jnp.bfloat16)], axis=1
    )
    picked = jnp.dot(pick, table, preferred_element_type=jnp.float32)
    at = jnp.sum((picked[:, :LANES] <= rest[:, None].astype(jnp.float32)).astype(jnp.int32), axis=1)
    kept = jnp.sum(
        jnp.where(jnp.arange(LANES)[None, :] == at[:, None], picked[:, LANES:], 0.0), axis=1
    )
    source = row * LANES + at
    source = (source % COLS) * HID + source // COLS
    return jnp.where(filled & (kept > 0.5), source, NBLK)


def kernel(
    u_ref, g_ref, w_ref, src_ref,
    pre_ref, out_ref,
    wg, wbuf, grad, act_t, slope, acc, send, stage,
    f1a, l1a, r1a, f1b, l1b, r1b, f2a, l2a, r2a, f2b, l2b, r2b,
    local_sem, w_sem, z_send, z_recv, s_send, s_recv, d_send, d_recv,
):
    dp = lax.axis_index("dp")
    mp = lax.axis_index("mp")
    y, x = dp // 4, lax.rem(dp, 4)
    z, core = mp // 2, lax.rem(mp, 2)

    def step(p, d):
        return lax.rem(p + d + 4, 4)

    z_right, z_left, z_far = step(z, 1), step(z, -1), step(z, 2)
    dev_z = ((dp, z_right * 2 + core), (dp, z_left * 2 + core))
    dev_sib = (dp, z * 2 + 1 - core)
    dev_x = ((y * 4 + step(x, 1), mp), (y * 4 + step(x, -1), mp))
    dev_y = ((step(y, 1) * 4 + x, mp), (step(y, -1) * 4 + x, mp))

    barrier = pltpu.get_barrier_semaphore()
    peers = (*dev_z, dev_sib, *dev_x, *dev_y)
    for peer in peers:
        pl.semaphore_signal(barrier, inc=1, device_id=peer, device_id_type=MESH)

    def w_load(zp, slot, sem):
        cols = pl.ds(pl.multiple_of(zp * PAIR, LANES), PAIR)
        return pltpu.make_async_copy(w_ref.at[:, cols], wbuf.at[slot], w_sem.at[sem])

    mine = pl.ds(pl.multiple_of(core * PART, LANES), PART)
    other = pl.ds(pl.multiple_of((1 - core) * PART, LANES), PART)
    own_copy = pltpu.make_async_copy(g_ref, grad.at[z, :, mine], local_sem.at[0])
    own_copy.start()
    loads = [w_load(z, 0, 0), w_load(z_left, 1, 1), w_load(z_right, 2, 2), w_load(z_far, 0, 3)]
    for load in loads[:3]:
        load.start()

    pl.semaphore_wait(barrier, len(peers))

    h0, h1 = pl.ds(0, HALF), pl.ds(HALF, HALF)

    def remote(src, dst, s_sem, r_sem, device):
        return pltpu.make_async_remote_copy(
            src_ref=src, dst_ref=dst, send_sem=s_sem, recv_sem=r_sem, device_id=device, device_id_type=MESH
        )

    def z_copy(n, src, zp, rows, way):
        return remote(src, grad.at[zp, rows, mine], z_send.at[n], z_recv.at[n], dev_z[way])

    def s_copy(n, zp, rows):
        part = grad.at[zp, rows, mine]
        return remote(part, part, s_send.at[n], s_recv.at[n], dev_sib)

    z_own = [
        z_copy(0, g_ref.at[h0], z, h0, 0),
        z_copy(1, g_ref.at[h1], z, h1, 1),
        z_copy(2, g_ref.at[h1], z, h1, 0),
        z_copy(3, g_ref.at[h0], z, h0, 1),
    ]
    s_own = remote(g_ref, grad.at[z, :, mine], s_send.at[0], s_recv.at[0], dev_sib)
    for copy in z_own:
        copy.start()
    s_own.start()
    z_fwd = [
        z_copy(4, grad.at[z_left, h0, mine], z_left, h0, 0),
        z_copy(5, grad.at[z_right, h1, mine], z_right, h1, 1),
    ]
    s_fwd = [
        s_copy(1, z_left, h0),
        s_copy(2, z_right, h1),
        s_copy(3, z_left, h1),
        s_copy(4, z_right, h0),
        s_copy(5, z_far, h0),
        s_copy(6, z_far, h1),
    ]

    wg[pl.ds(NBLK, GROUP), :] = jnp.zeros((GROUP, LANES), jnp.float32)

    def gelu(n, carry):
        tok = pl.ds(pl.multiple_of(lax.rem(n, 4) * LANES, LANES), LANES)
        hid = pl.ds(pl.multiple_of((n // 4) * LANES, LANES), LANES)
        values = u_ref[tok, hid].astype(jnp.float32)
        cdf = 0.5 * (1.0 + lax.erf(values * half_root))
        density = jnp.exp(-0.5 * values * values) * inv_root_tau
        act_t[hid, tok] = (values * cdf).T.astype(jnp.bfloat16)
        slope[tok, hid] = cdf + values * density
        return carry

    lax.fori_loop(0, 4 * (HID // LANES), gelu, 0)

    def weight_grad(zp, n, part_cols, width):
        cols = pl.ds(pl.multiple_of(part_cols + n * width, LANES), width)
        first = zp * (PAIR // LANES) + (part_cols + n * width) // LANES
        for half in range(2):
            product = jnp.dot(
                act_t[pl.ds(half * PART, PART), :], grad[zp, :, cols], preferred_element_type=jnp.float32
            )
            for c in range(width // LANES):
                row = pl.multiple_of((first + c) * HID + half * PART, LANES)
                wg[pl.ds(row, PART), :] = product[:, c * LANES : (c + 1) * LANES]

    def weight_grad_pair(zp):
        def body(n, carry):
            weight_grad(zp, n, 0, 256)
            return carry

        lax.fori_loop(0, PAIR // 256, body, 0)

    def weight_grad_part(zp, which):
        def body(n, carry):
            weight_grad(zp, n, which * PART, LANES)
            return carry

        lax.fori_loop(0, PART // LANES, body, 0)

    def pre_product(zp, slot, rows, mode):
        def body(n, carry):
            hid = pl.ds(pl.multiple_of(n * 256, LANES), 256)
            product = lax.dot_general(
                grad[zp, rows, :], wbuf[slot, hid, :], (((1,), (1,)), ((), ())),
                preferred_element_type=jnp.float32,
            )
            if mode == "first":
                acc[rows, hid] = product
            elif mode == "add":
                acc[rows, hid] += product
            else:
                pre_ref[rows, hid] = ((acc[rows, hid] + product) * slope[rows, hid]).astype(jnp.bfloat16)
            return carry

        lax.fori_loop(0, HID // 256, body, 0)

    whole = pl.ds(0, TOK)
    own_copy.wait()
    s_own.wait_recv()
    weight_grad_pair(z)
    loads[0].wait()
    pre_product(z, 0, whole, "first")
    loads[3].start()
    z_own[0].wait_recv()
    z_fwd[0].start()
    s_fwd[0].start()
    z_own[1].wait_recv()
    z_fwd[1].start()
    s_fwd[1].start()
    loads[1].wait()
    loads[2].wait()
    s_fwd[0].wait_recv()
    pre_product(z_left, 1, h0, "add")
    s_fwd[1].wait_recv()
    pre_product(z_right, 2, h1, "add")
    z_own[2].wait_recv()
    s_fwd[2].start()
    z_own[3].wait_recv()
    s_fwd[3].start()
    s_fwd[2].wait_recv()
    weight_grad_pair(z_left)
    s_fwd[3].wait_recv()
    weight_grad_pair(z_right)
    pre_product(z_left, 1, h1, "add")
    pre_product(z_right, 2, h0, "add")
    z_fwd[0].wait_recv()
    s_fwd[4].start()
    z_fwd[1].wait_recv()
    s_fwd[5].start()
    weight_grad_part(z_far, core)
    s_fwd[4].wait_recv()
    s_fwd[5].wait_recv()
    weight_grad_part(z_far, 1 - core)

    scale = 1.0 / math.sqrt(TOK * 16)

    def gather(half, q, row, count):
        groups = count // GROUP

        def body(n, carry):
            p = n // groups
            at = pl.multiple_of(row + (n - p * groups) * GROUP, GROUP)
            ry, rx = (p, q) if half == 0 else (q, p)
            first = (ry * 4 + rx) * KEEP + at
            buf = lax.rem(n, 2)
            for s in range(GROUP):
                stage[buf, pl.ds(s, 1), :] = wg[pl.ds(src_ref[first + s], 1), :]
            send[ry, rx, pl.ds(at, GROUP), :] = (stage[buf] * scale).astype(jnp.bfloat16)
            return carry

        lax.fori_loop(0, 4 * groups, body, 0)

    def many(buf, half, q, row, count):
        return buf.at[:, q, pl.ds(row, count)] if half == 0 else buf.at[q, :, pl.ds(row, count)]

    def one(buf, half, q, row, count):
        return buf.at[q, x, pl.ds(row, count)] if half == 0 else buf.at[y, q, pl.ds(row, count)]

    bufs = (
        ((f1a, l1a, r1a), (f2a, l2a, r2a)),
        ((f1b, l1b, r1b), (f2b, l2b, r2b)),
    )

    def scatter_copies(half, level):
        low, a, b = SPLIT[half]
        fwd, left, right = bufs[half][level]
        along_x = half == level
        devices = dev_x if along_x else dev_y
        here = x if along_x else y
        pick = many if level == 0 else one
        base = 20 * half + 6 * level

        def sub(buf, row, count):
            return buf.at[:, pl.ds(row, count)] if level == 0 else buf.at[pl.ds(row, count)]

        def copy(n, q, row, count, dst, way):
            return remote(
                pick(send, half, q, low + row, count), sub(dst, row, count),
                d_send.at[base + n], d_recv.at[base + n], devices[way],
            )

        nxt, prv, far = step(here, 1), step(here, -1), step(here, 2)
        return (
            copy(0, far, 0, a, fwd, 0),
            copy(1, far, a, b, fwd, 1),
            copy(2, nxt, a, b, left, 0),
            copy(3, prv, 0, a, right, 1),
            copy(4, nxt, 0, a, left, 0),
            copy(5, prv, a, b, right, 1),
        ), (nxt, prv, far, here)

    def add_forward(half, level, places, way):
        low, a, b = SPLIT[half]
        fwd = bufs[half][level][0]
        row, count = (0, a) if way == 0 else (a, b)
        q = places[way]
        if level == 0:
            def body(p, carry):
                ry, rx = (p, q) if half == 0 else (q, p)
                rows = pl.ds(low + row, count)
                send[ry, rx, rows, :] = (
                    send[ry, rx, rows, :].astype(jnp.float32) + fwd[p, pl.ds(row, count), :].astype(jnp.float32)
                ).astype(jnp.bfloat16)
                return carry

            lax.fori_loop(0, 4, body, 0)
        else:
            ry, rx = (q, x) if half == 0 else (y, q)
            rows = pl.ds(low + row, count)
            send[ry, rx, rows, :] = (
                send[ry, rx, rows, :].astype(jnp.float32) + fwd[pl.ds(row, count), :].astype(jnp.float32)
            ).astype(jnp.bfloat16)

    def add_own(half, level):
        low, a, b = SPLIT[half]
        _, left, right = bufs[half][level]
        rows = pl.ds(low, a + b)
        if level == 0:
            def body(p, carry):
                ry, rx = (p, x) if half == 0 else (y, p)
                send[ry, rx, rows, :] = (
                    send[ry, rx, rows, :].astype(jnp.float32)
                    + left[p].astype(jnp.float32)
                    + right[p].astype(jnp.float32)
                ).astype(jnp.bfloat16)
                return carry

            lax.fori_loop(0, 4, body, 0)
        else:
            out_ref[y, x, rows, :] = (
                send[y, x, rows, :].astype(jnp.float32)
                + left[...].astype(jnp.float32)
                + right[...].astype(jnp.float32)
            ).astype(jnp.bfloat16)

    first = [scatter_copies(half, 0) for half in range(2)]
    second = [scatter_copies(half, 1) for half in range(2)]
    for half in range(2):
        low, a, b = SPLIT[half]
        copies, (nxt, prv, far, here) = first[half]
        gather(half, far, low, a + b)
        copies[0].start()
        copies[1].start()
    for half in range(2):
        low, a, b = SPLIT[half]
        copies, (nxt, prv, far, here) = first[half]
        gather(half, nxt, low + a, b)
        copies[2].start()
        gather(half, prv, low, a)
        copies[3].start()
    for half in range(2):
        low, a, b = SPLIT[half]
        copies, (nxt, prv, far, here) = first[half]
        gather(half, nxt, low, a)
        copies[0].wait_recv()
        add_forward(half, 0, (nxt, prv), 0)
        copies[4].start()
        gather(half, prv, low + a, b)
        copies[1].wait_recv()
        add_forward(half, 0, (nxt, prv), 1)
        copies[5].start()
    for half in range(2):
        low, a, b = SPLIT[half]
        gather(half, first[half][1][3], low, a + b)

    loads[3].wait()
    pre_product(z_far, 0, whole, "last")

    for half in range(2):
        for n in range(2, 6):
            first[half][0][n].wait_recv()
        add_own(half, 0)
        for n in range(4):
            second[half][0][n].start()
    for half in range(2):
        copies, (nxt, prv, far, here) = second[half]
        for way in range(2):
            copies[way].wait_recv()
            add_forward(half, 1, (nxt, prv), way)
            copies[4 + way].start()

    def gather_copies(half, level):
        low, a, b = SPLIT[half]
        along_x = half == 1 - level
        devices = dev_x if along_x else dev_y
        here = x if along_x else y
        pick = one if level == 0 else many
        base = 20 * half + 12 + 4 * level

        def copy(n, q, row, count, way):
            part = pick(out_ref, half, q, low + row, count)
            return remote(part, part, d_send.at[base + n], d_recv.at[base + n], devices[way])

        nxt, prv = step(here, 1), step(here, -1)
        return (
            copy(0, here, 0, a + b, 0),
            copy(1, here, 0, a + b, 1),
            copy(2, prv, 0, a, 0),
            copy(3, nxt, a, b, 1),
        )

    third = [gather_copies(half, 0) for half in range(2)]
    fourth = [gather_copies(half, 1) for half in range(2)]
    for half in range(2):
        for n in range(2, 6):
            second[half][0][n].wait_recv()
        add_own(half, 1)
        third[half][0].start()
        third[half][1].start()
    for half in range(2):
        for n in range(2):
            third[half][n].wait_recv()
            third[half][2 + n].start()
    for half in range(2):
        third[half][2].wait_recv()
        third[half][3].wait_recv()
        fourth[half][0].start()
        fourth[half][1].start()
    for half in range(2):
        for n in range(2):
            fourth[half][n].wait_recv()
            fourth[half][2 + n].start()
    for half in range(2):
        fourth[half][2].wait_recv()
        fourth[half][3].wait_recv()

    for copy in (*z_own, s_own, *z_fwd, *s_fwd):
        copy.wait_send()
    for half in range(2):
        for copy in (*first[half][0], *second[half][0], *third[half], *fourth[half]):
            copy.wait_send()


def fused(u, grad_part, weights, source):
    rows_a = SPLIT[0][1] + SPLIT[0][2]
    rows_b = SPLIT[1][1] + SPLIT[1][2]
    big = [pltpu.VMEM((4, rows, LANES), jnp.bfloat16) for rows in (rows_a, rows_b) for _ in range(3)]
    small = [pltpu.VMEM((rows, LANES), jnp.bfloat16) for rows in (rows_a, rows_b) for _ in range(3)]
    vmem = pl.BlockSpec(memory_space=pltpu.VMEM)
    hbm = pl.BlockSpec(memory_space=pl.ANY)
    return pl.pallas_call(
        kernel,
        out_shape=(
            jax.ShapeDtypeStruct((TOK, HID), jnp.bfloat16),
            jax.ShapeDtypeStruct((4, 4, KEEP, LANES), jnp.bfloat16),
        ),
        in_specs=[vmem, hbm, hbm, pl.BlockSpec(memory_space=pltpu.SMEM)],
        out_specs=(vmem, vmem),
        scratch_shapes=[
            pltpu.VMEM((NBLK + GROUP, LANES), jnp.float32),
            pltpu.VMEM((3, HID, PAIR), jnp.bfloat16),
            pltpu.VMEM((4, TOK, PAIR), jnp.bfloat16),
            pltpu.VMEM((HID, TOK), jnp.bfloat16),
            pltpu.VMEM((TOK, HID), jnp.float32),
            pltpu.VMEM((TOK, HID), jnp.float32),
            pltpu.VMEM((4, 4, KEEP, LANES), jnp.bfloat16),
            pltpu.VMEM((2, GROUP, LANES), jnp.float32),
            *big,
            *small,
            pltpu.SemaphoreType.DMA((1,)),
            pltpu.SemaphoreType.DMA((4,)),
            pltpu.SemaphoreType.DMA((6,)),
            pltpu.SemaphoreType.DMA((6,)),
            pltpu.SemaphoreType.DMA((7,)),
            pltpu.SemaphoreType.DMA((7,)),
            pltpu.SemaphoreType.DMA((40,)),
            pltpu.SemaphoreType.DMA((40,)),
        ],
        compiler_params=pltpu.CompilerParams(
            collective_id=0, has_side_effects=True, vmem_limit_bytes=62 * 1024 * 1024
        ),
        cost_estimate=pl.CostEstimate(
            flops=4 * TOK * HID * WIDTH, bytes_accessed=20_000_000, transcendentals=2 * TOK * HID
        ),
    )(u, grad_part, weights, source)


def local(
    inner_before_nonlinear,
    layer_exit_derivative,
    contract_weights,
    copy_tile_indicator,
    span_opening_tile,
    remaining_tile_flags,
):
    source = slot_sources(remaining_tile_flags[0], copy_tile_indicator[0, 0], span_opening_tile)
    pre_grad, sums = fused(inner_before_nonlinear, layer_exit_derivative, contract_weights, source)
    return (pre_grad, sums.reshape(1, 16 * KEEP, LANES).astype(jnp.float32))


def solution(mesh):
    in_specs = (
        P("dp", "mp"),
        P("dp", "mp"),
        P("mp", None),
        P("dp", "mp", None),
        P(),
        P("mp", None),
    )
    out_specs = (P("dp", "mp"), P("mp", None, None))
    return jax.shard_map(local, mesh=mesh, in_specs=in_specs, out_specs=out_specs, check_vma=False)
```

time: 414 us -> 101 us (0.24)
  waiting for transfers between devices: 187 us -> 0 us
  local copies, waits for them, and re-layouts: 104 us -> 1.48 us
  Pallas kernels: 0 us -> 82.7 us
  other arithmetic: 77.7 us -> 11.9 us
  matrix products: 26.9 us -> 2.51 us
  between operations: 17.1 us -> 0.71 us
    reduce_scatter x1 -> x0, waiting for transfers between devices: 118 us -> none  [local(): lax.psum_scatter(dense_term, 'dp', scatter_dimension=0, tiled=True)]
    pallas_call x0 -> x1, Pallas kernels: none -> 82.7 us  [fused(): pl.pallas_call(kernel, out_shape=(jax.ShapeDtypeStruct((TOK, HID), jnp.bf...]
    select_n x3 -> x1, other arithmetic: 69 us -> 0.65 us  [slot_sources(): return jnp.where(filled & (kept > 0.5), source, NBLK)]
    all_gather x2 -> x0, waiting for transfers between devices: 68.1 us -> none  [the longest x1 38.2 us: local(): full_grad = lax.all_gather(layer_exit_derivative, 'mp', axis=1, tiled=True)]
    gather x49 -> x0, local copies, waits for them, and re-layouts: 65.1 us -> none
    dot_general x2, matrix products: 26.9 us -> 2.51 us  [the longest x1 2.34 us: slot_sources(): picked = jnp.dot(pick, table, preferred_element_type=jnp.float32)]
    reshape x1 -> x0, local copies, waits for them, and re-layouts: 19.7 us -> none  [local(): grad_rows = weight_grad.reshape(blocks_local, 128)]
    concatenate x2 -> x0, local copies, waits for them, and re-layouts: 17.2 us -> none  [the longest x1 17.2 us: local(): jnp.concatenate([masked, jnp.zeros((widest_span_tally, 128), jnp.bfloat16...]
  transfers between devices with their start and end apart: 3 -> 0, of which waited for: 3 -> 0; matrix products, arithmetic and copies ran while one was open for 5% -> 0% of each run, Pallas kernels for 0% -> 0%
where the time goes in v1:
time: 101 us; the launch traced here: 99.3 us
  Pallas kernels  82.7 us (82%)
  other arithmetic  11.9 us (12%)
  matrix products  2.51 us (2%)
  local copies, waits for them, and re-layouts  1.48 us (1%)
    pallas_call x1, Pallas kernels, fused(): pl.pallas_call(kernel, out_shape=(jax.ShapeDtypeStruct((TOK, HID), jnp.bf...  82.7 us
    convert_element_type x1, other arithmetic, local(): return (pre_grad, sums.reshape(1, 16 * KEEP, LANES).astype(jnp.float32))  3.45 us
    dot_general x1, matrix products, slot_sources(): picked = jnp.dot(pick, table, preferred_element_type=jnp.float32)  2.34 us

profile of v1, /device:TPU:0, one launch (start us, length us, event | category | flops | bytes accessed | tf_op | source)
XLA Modules:
  0.0 99.3 jit_solution(9373066760642725887)
XLA Ops:
  0.6 1.7 %select_reduce_fusion = s32[17]{0:T(128)S(1)} fusion(s32[51200]{0:T(1024)} %bitcast.17, s32[17]{0:T(128)} %param.10), kind=kLoop, calls=%fused_computation.7 | loop fusion | flops 2611183 | bytes 204936 | tf_op jit(solution)/shard_map/reduce_sum | solution.py:42
  2.3 0.1 slice_subtract_fusion
  2.4 0.1 iota_compare_fusion.5
  2.5 0.1 lt.57
  2.6 0.1 iota_add_fusion
  2.7 0.1 add.45
  2.7 1.5 %convert_reduce_fusion.1 = bf16[51200]{0:T(1024)(128)(2,1)S(1)} fusion(s32[1,1,51200]{2,1,0:T(1,128)} %param.9), kind=kLoop, calls=%fused_computation.21 | loop fusion | flops 51200 | bytes 307200 | tf_op jit(solution)/shard_map/convert_element_type | solution.py:51
  4.2 1.5 %convert_reduce_fusion.2 = bf16[51200]{0:T(1024)(128)(2,1)S(1)} fusion(s32[1,51200]{1,0:T(1,128)} %param.11), kind=kLoop, calls=%fused_computation.22 | loop fusion | flops 51200 | bytes 307200 | tf_op jit(solution)/shard_map/convert_element_type | solution.py:34
  5.7 0.2 fusion.14
  5.9 0.2 slice_reduce_fusion
  6.1 0.2 select_reduce_fusion.1
  6.3 2.0 %fusion.1 = (s32[6400]{0:T(1024)S(1)}, s32[6400]{0:T(1024)S(1)}) fusion(s32[400]{0:T(512)S(1)} %get-tuple-element.9, s32[6400]{0:T(1024)S(1)} %add.45, s32[400]{0:T(512)S(1)} %get-tuple-element.8), kind=kLoop, calls=%fused_computation.3 | loop fusion | flops 12787200 | bytes 80000 | tf_op jit(solution)/shard_map/reduce_sum | solution.py:48
  8.3 2.3 %fusion.2 = f32[6400,256]{0,1:T(8,128)S(1)} fusion(s32[6400]{0:T(1024)S(1)} %get-tuple-element.7, bf16[400,128]{1,0:T(8,128)(2,1)S(1)} %bitcast.18, bf16[400,128]{1,0:T(8,128)(2,1)S(1)} %get-tuple-element.12), kind=kOutput, calls=%fused_computation.5 | convolution fusion | flops 1313689600 | bytes 6784000 | tf_op jit(solution)/shard_map/dot_general | solution.py:53
  10.6 0.4 convert_reduce_fusion
  11.0 0.4 fusion.4
  11.4 0.7 fusion.11.src_ref
  12.1 82.7 %shard_map.77 = (bf16[512,1280]{1,0:T(8,128)(2,1)}, bf16[4,4,400,128]{3,2,1,0:T(8,128)(2,1)}) custom-call(bf16[512,1280]{1,0:T(8,128)(2,1)} %u_ref.1, bf16[512,640]{1,0:T(8,128)(2,1)} %g_ref.1, bf16[1280,5120]{1,0:T(8,128)(2,1)} %w_ref.1, s32[6400]{0:T(1024)} %fusion.11.src_ref), custom_call_target="tpu_custom_call" | custom-call | flops 13421772800 | bytes 20000000 | tf_op jit(solution)/shard_map/pallas_call | solution.py:440
  94.8 0.0 copy-start
  94.8 3.5 %convert.1 = f32[1,6400,128]{2,1,0:T(8,128)} convert(bf16[1,6400,128]{2,1,0:T(8,128)(2,1)} %bitcast.16) | non-fusion elementwise | flops 819200 | bytes 4915200 | tf_op jit(solution)/shard_map/convert_element_type | solution.py:487
  98.3 0.0 copy-done
  98.3 1.1 %copy.9 = bf16[512,1280]{1,0:T(8,128)(2,1)} copy(bf16[512,1280]{1,0:T(8,128)(2,1)S(1)} %copy-done) | data formatting | bytes 2621440
  (2 shorter events, 0.0 us)
Async XLA Ops:
  94.8 3.5 %copy-start = (bf16[512,1280]{1,0:T(8,128)(2,1)S(1)}, bf16[512,1280]{1,0:T(8,128)(2,1)}, u32[]{:S(2)}) copy-start(bf16[512,1280]{1,0:T(8,128)(2,1)} %get-tuple-element.16) | copy-start | bytes 3932164

commit v2 on v1

v2 whole, which is shorter than its diff:
```python
import functools
import math

import jax
import jax.numpy as jnp
from jax import lax
from jax.experimental import pallas as pl
from jax.experimental.pallas import tpu as pltpu
from jax.sharding import PartitionSpec as P

half_root = 0.7071067811865476
inv_root_tau = 0.3989422804014327
MESH = pl.DeviceIdType.MESH

TOK = 512
HID = 1280
WIDTH = 5120
PART = 640
PAIR = 2 * PART
LANES = 128
COLS = WIDTH // LANES
NBLK = HID * COLS
KEEP = 400
HALF = TOK // 2
GROUP = 16
ROWS = NBLK // LANES
ROWS_PAD = 448
WINDOW = 48
SLOTS = 512
CUT = 384
SPLIT = ((0, 112, 96), (208, 96, 96))


def index_kernel(flag_ref, copied_ref, start_ref, src_ref, flags, copied, within, upto, before, opening):
    flags[pl.ds(0, ROWS), :] = flag_ref[...]
    copied[pl.ds(0, ROWS), :] = copied_ref[...].astype(jnp.float32)
    pad = pl.ds(ROWS, ROWS_PAD - ROWS)
    flags[pad, :] = jnp.zeros((ROWS_PAD - ROWS, LANES), jnp.int32)
    copied[pad, :] = jnp.zeros((ROWS_PAD - ROWS, LANES), jnp.float32)

    def iota(shape, dim):
        return lax.broadcasted_iota(jnp.int32, shape, dim)

    square = (LANES, LANES)
    flag_bf = flags[...].astype(jnp.float32).astype(jnp.bfloat16)
    tri = jnp.where(iota(square, 0) <= iota(square, 1), 1.0, 0.0).astype(jnp.bfloat16)
    within[...] = jnp.dot(flag_bf, tri, preferred_element_type=jnp.float32)
    totals = jnp.dot(flag_bf, jnp.ones(square, jnp.bfloat16), preferred_element_type=jnp.float32)
    tall = (ROWS_PAD, ROWS_PAD)
    tri = jnp.where(iota(tall, 0) >= iota(tall, 1), 1.0, 0.0).astype(jnp.bfloat16)
    sums = jnp.dot(tri, totals.astype(jnp.bfloat16), preferred_element_type=jnp.float32)
    upto[...] = sums
    before[...] = sums - totals
    for o in range(17):
        start = start_ref[o]
        row = pl.ds(lax.shift_right_logical(start, 7), 1)
        inside = jnp.where(iota((1, LANES), 1) < lax.bitwise_and(start, 127), flags[row, :], 0).astype(jnp.float32)
        opening[pl.ds(o, 1), :] = before[row, :] + jnp.sum(inside, axis=1, keepdims=True)

    def wide(v):
        return jnp.concatenate([v] * (SLOTS // LANES), axis=1)

    def sources(o):
        row0 = pl.multiple_of(lax.bitwise_and(lax.shift_right_logical(start_ref[o], 7), -8), 8)
        rows = pl.ds(row0, WINDOW)
        target = wide(opening[pl.ds(o, 1), :]) + iota((1, SLOTS), 1).astype(jnp.float32)
        limit = wide(opening[pl.ds(o + 1, 1), :])
        ends = wide(upto[rows, :])
        passed = ends <= target
        count = jnp.sum(jnp.where(passed, 1.0, 0.0), axis=0, keepdims=True)
        last = jnp.max(jnp.where(passed, ends, wide(before[pl.ds(row0, 1), :])), axis=0, keepdims=True)
        pick = jnp.where(iota((WINDOW, SLOTS), 0).astype(jnp.float32) == count, 1.0, 0.0).astype(jnp.bfloat16)

        def lookup(table):
            return lax.dot_general(
                table.astype(jnp.bfloat16), pick, (((0,), (0,)), ((), ())), preferred_element_type=jnp.float32
            )

        at = jnp.sum(jnp.where(lookup(within[rows, :]) <= target - last, 1.0, 0.0), axis=0, keepdims=True)
        here = iota((LANES, SLOTS), 0).astype(jnp.float32) == at
        kept = jnp.sum(
            jnp.where(here, lookup(copied[rows, :]), 0.0), axis=0, keepdims=True
        )
        block = (count + row0.astype(jnp.float32)) * LANES + at
        hid = jnp.floor((block + 0.5) * (1.0 / COLS))
        source = (block - hid * COLS) * HID + hid
        source = jnp.where((target < limit) & (kept > 0.5), source, float(NBLK))
        src_ref[:, pl.ds(o * SLOTS, SLOTS)] = source.astype(jnp.int32)

    for o in range(16):
        sources(o)


def slot_sources(flags, copied, starts):
    vmem = pl.BlockSpec(memory_space=pltpu.VMEM)
    table = pltpu.VMEM((ROWS_PAD, LANES), jnp.float32)
    return pl.pallas_call(
        index_kernel,
        out_shape=jax.ShapeDtypeStruct((1, 16 * SLOTS), jnp.int32),
        in_specs=[vmem, vmem, pl.BlockSpec(memory_space=pltpu.SMEM)],
        out_specs=vmem,
        scratch_shapes=[
            pltpu.VMEM((ROWS_PAD, LANES), jnp.int32),
            table,
            table,
            table,
            table,
            pltpu.VMEM((24, LANES), jnp.float32),
        ],
    )(flags, copied, starts)


def kernel(
    u_ref, g_ref, w_ref, src_ref,
    pre_out, out_ref,
    wg, wbuf, grad, act_t, slope, acc, send_a, send_b, u_buf, pre_ref,
    f1a, l1a, r1a, f1b, l1b, r1b, f2a, l2a, r2a, f2b, l2b, r2b,
    local_sem, w_sem, z_send, z_recv, s_send, s_recv, d_send, d_recv,
):
    dp = lax.axis_index("dp")
    mp = lax.axis_index("mp")
    y, x = dp // 4, lax.rem(dp, 4)
    z, core = mp // 2, lax.rem(mp, 2)

    def step(p, d):
        return lax.rem(p + d + 4, 4)

    z_right, z_left, z_far = step(z, 1), step(z, -1), step(z, 2)
    dev_z = ((dp, z_right * 2 + core), (dp, z_left * 2 + core))
    dev_sib = (dp, z * 2 + 1 - core)
    dev_x = ((y * 4 + step(x, 1), mp), (y * 4 + step(x, -1), mp))
    dev_y = ((step(y, 1) * 4 + x, mp), (step(y, -1) * 4 + x, mp))

    barrier = pltpu.get_barrier_semaphore()
    peers = (*dev_z, dev_sib, *dev_x, *dev_y, (y * 4 + step(x, 2), mp), (step(y, 2) * 4 + x, mp))
    for peer in peers:
        pl.semaphore_signal(barrier, inc=1, device_id=peer, device_id_type=MESH)

    def w_load(zp, slot, sem):
        cols = pl.ds(pl.multiple_of(zp * PAIR, LANES), PAIR)
        return pltpu.make_async_copy(w_ref.at[:, cols], wbuf.at[slot], w_sem.at[sem])

    mine = pl.ds(pl.multiple_of(core * PART, LANES), PART)
    other = pl.ds(pl.multiple_of((1 - core) * PART, LANES), PART)
    own_copy = pltpu.make_async_copy(g_ref, grad.at[z, :, mine], local_sem.at[0])
    u_copy = pltpu.make_async_copy(u_ref, u_buf, local_sem.at[1])
    u_copy.start()
    own_copy.start()
    loads = [w_load(z, 0, 0), w_load(z_left, 1, 1), w_load(z_right, 2, 2), w_load(z_far, 0, 3)]
    pl.semaphore_wait(barrier, len(peers))

    h0, h1 = pl.ds(0, HALF), pl.ds(HALF, HALF)

    def remote(src, dst, s_sem, r_sem, device):
        return pltpu.make_async_remote_copy(
            src_ref=src, dst_ref=dst, send_sem=s_sem, recv_sem=r_sem, device_id=device, device_id_type=MESH
        )

    def z_copy(n, src, zp, rows, way):
        return remote(src, grad.at[zp, rows, mine], z_send.at[n], z_recv.at[n], dev_z[way])

    def piece(zp, rows, col, width):
        return grad.at[zp, rows, pl.ds(pl.multiple_of(core * PART + col, LANES), width)]

    def z_pass(n, zp, rows, col, width, way):
        part = piece(zp, rows, col, width)
        return remote(part, part, z_send.at[n], z_recv.at[n], dev_z[way])

    def s_copy(n, zp, rows, col=0, width=PART):
        part = piece(zp, rows, col, width)
        return remote(part, part, s_send.at[n], s_recv.at[n], dev_sib)

    z_own = [
        z_copy(0, g_ref.at[h0], z, h0, 0),
        z_copy(1, g_ref.at[h1], z, h1, 1),
        z_copy(2, g_ref.at[h1], z, h1, 0),
        z_copy(3, g_ref.at[h0], z, h0, 1),
    ]
    s_own = remote(g_ref, grad.at[z, :, mine], s_send.at[0], s_recv.at[0], dev_sib)
    z_own[0].start()
    z_own[1].start()
    s_own.start()
    z_fwd = [
        z_pass(4, z_left, h0, 0, CUT, 0),
        z_pass(5, z_right, h1, 0, CUT, 1),
        z_pass(6, z_left, h0, CUT, PART - CUT, 0),
        z_pass(7, z_right, h1, CUT, PART - CUT, 1),
    ]
    s_fwd = [
        s_copy(1, z_left, h0),
        s_copy(2, z_right, h1),
        s_copy(3, z_left, h1),
        s_copy(4, z_right, h0),
        s_copy(5, z_far, h0, 0, CUT),
        s_copy(6, z_far, h1, 0, CUT),
        s_copy(7, z_far, h0, CUT, PART - CUT),
        s_copy(8, z_far, h1, CUT, PART - CUT),
    ]

    wg[pl.ds(NBLK, GROUP), :] = jnp.zeros((GROUP, LANES), jnp.float32)

    u_copy.wait()
    for load in loads[:3]:
        load.start()

    def gelu(n, carry):
        tok = pl.ds(pl.multiple_of(lax.rem(n, 4) * LANES, LANES), LANES)
        hid = pl.ds(pl.multiple_of((n // 4) * LANES, LANES), LANES)
        values = u_buf[tok, hid].astype(jnp.float32)
        cdf = 0.5 * (1.0 + lax.erf(values * half_root))
        density = jnp.exp(-0.5 * values * values) * inv_root_tau
        act_t[hid, tok] = (values * cdf).T.astype(jnp.bfloat16)
        slope[tok, hid] = cdf + values * density
        return carry

    lax.fori_loop(0, 4 * (HID // LANES), gelu, 0)

    def weight_grad(zp, n, part_cols, width):
        cols = pl.ds(pl.multiple_of(part_cols + n * width, LANES), width)
        first = zp * (PAIR // LANES) + (part_cols + n * width) // LANES
        for half in range(2):
            product = jnp.dot(
                act_t[pl.ds(half * PART, PART), :], grad[zp, :, cols], preferred_element_type=jnp.float32
            )
            for c in range(width // LANES):
                row = pl.multiple_of((first + c) * HID + half * PART, LANES)
                wg[pl.ds(row, PART), :] = product[:, c * LANES : (c + 1) * LANES]

    def weight_grad_pair(zp):
        def body(n, carry):
            weight_grad(zp, n, 0, 256)
            return carry

        lax.fori_loop(0, PAIR // 256, body, 0)

    def pre_product(zp, slot, rows, mode):
        def body(n, carry):
            hid = pl.ds(pl.multiple_of(n * 256, LANES), 256)
            product = lax.dot_general(
                grad[zp, rows, :], wbuf[slot, hid, :], (((1,), (1,)), ((), ())),
                preferred_element_type=jnp.float32,
            )
            if mode == "first":
                acc[rows, hid] = product
            elif mode == "add":
                acc[rows, hid] += product
            else:
                pre_ref[rows, hid] = ((acc[rows, hid] + product) * slope[rows, hid]).astype(jnp.bfloat16)
            return carry

        lax.fori_loop(0, HID // 256, body, 0)

    whole = pl.ds(0, TOK)
    own_copy.wait()
    s_own.wait_recv()
    weight_grad_pair(z)
    z_own[2].start()
    z_own[3].start()
    loads[0].wait()
    pre_product(z, 0, whole, "first")
    loads[3].start()
    z_own[0].wait_recv()
    s_fwd[0].start()
    z_own[1].wait_recv()
    s_fwd[1].start()
    loads[1].wait()
    loads[2].wait()
    s_fwd[0].wait_recv()
    pre_product(z_left, 1, h0, "add")
    s_fwd[1].wait_recv()
    pre_product(z_right, 2, h1, "add")
    z_fwd[0].start()
    z_fwd[1].start()
    z_own[2].wait_recv()
    s_fwd[2].start()
    z_own[3].wait_recv()
    s_fwd[3].start()
    z_fwd[2].start()
    z_fwd[3].start()
    s_fwd[2].wait_recv()
    weight_grad_pair(z_left)
    z_fwd[0].wait_recv()
    s_fwd[4].start()
    z_fwd[1].wait_recv()
    s_fwd[5].start()
    s_fwd[3].wait_recv()
    weight_grad_pair(z_right)
    weight_grad(z_far, 0, core * PART, CUT)
    for way in range(2):
        s_fwd[4 + way].wait_recv()
    weight_grad(z_far, 0, (1 - core) * PART, CUT)
    for way in range(2):
        z_fwd[2 + way].wait_recv()
        s_fwd[6 + way].start()
    weight_grad(z_far, 0, core * PART + CUT, PART - CUT)
    for way in range(2):
        s_fwd[6 + way].wait_recv()
    weight_grad(z_far, 0, (1 - core) * PART + CUT, PART - CUT)

    scale = 1.0 / math.sqrt(TOK * 16)
    FAR, NEXT, PREV, OWN = range(4)
    SHIFT = (2, 1, -1, 0)
    parts = ((FAR, NEXT), (PREV, OWN))
    send = (send_a, send_b)
    bufs = (
        ((f1a, l1a, r1a), (f2a, l2a, r2a)),
        ((f1b, l1b, r1b), (f2b, l2b, r2b)),
    )

    def axis(half, level):
        along_x = half == level
        places = tuple(step(x if along_x else y, shift) for shift in SHIFT)
        devices = tuple((y * 4 + p, mp) if along_x else (p * 4 + x, mp) for p in places)
        return places, devices

    def gather(half, part, place, row, count):
        low = SPLIT[half][0]
        groups = count // GROUP
        one = axis(half, 0)[0][place]
        for second in parts[part]:
            two = axis(half, 1)[0][second]
            region = two * 4 + one if half == 0 else one * 4 + two

            def body(n, carry):
                at = pl.multiple_of(row + n * GROUP, GROUP)
                first = region * SLOTS + low + at
                taken = [wg[pl.ds(src_ref[0, first + s], 1), :] for s in range(GROUP)]
                send[half][second, place, pl.ds(at, GROUP), :] = (
                    jnp.concatenate(taken, axis=0) * scale
                ).astype(jnp.bfloat16)
                return carry

            lax.fori_loop(0, groups, body, 0)

    def scatter_first(half, part):
        _, a, b = SPLIT[half]
        fwd, left, right = bufs[half][0]
        devices = axis(half, 0)[1]
        lead = pl.ds(2 * part, 2)
        base = 32 * half + 6 * part

        def copy(n, place, row, count, dst, way):
            return remote(
                send[half].at[lead, place, pl.ds(row, count)], dst.at[lead, pl.ds(row, count)],
                d_send.at[base + n], d_recv.at[base + n], devices[way],
            )

        return (
            copy(0, FAR, 0, a, fwd, NEXT),
            copy(1, FAR, a, b, fwd, PREV),
            copy(2, NEXT, a, b, left, NEXT),
            copy(3, PREV, 0, a, right, PREV),
            copy(4, NEXT, 0, a, left, NEXT),
            copy(5, PREV, a, b, right, PREV),
        )

    def scatter_second(half):
        devices = axis(half, 1)[1]
        far, left, right = bufs[half][1]

        def copy(n, place, dst):
            return remote(
                send[half].at[place, OWN], dst,
                d_send.at[32 * half + 12 + n], d_recv.at[32 * half + 12 + n], devices[place],
            )

        return (copy(0, FAR, far), copy(1, NEXT, left), copy(2, PREV, right))

    def add_forward(half, part, way):
        _, a, b = SPLIT[half]
        fwd = bufs[half][0][0]
        row, count, place = ((0, a, NEXT), (a, b, PREV))[way]
        rows = pl.ds(row, count)
        for second in parts[part]:
            send[half][second, place, rows, :] = (
                send[half][second, place, rows, :].astype(jnp.float32) + fwd[second, rows, :].astype(jnp.float32)
            ).astype(jnp.bfloat16)

    def add_first(half, part):
        _, left, right = bufs[half][0]
        for second in parts[part]:
            send[half][second, OWN] = (
                send[half][second, OWN].astype(jnp.float32)
                + left[second].astype(jnp.float32)
                + right[second].astype(jnp.float32)
            ).astype(jnp.bfloat16)

    def add_second(half):
        low, a, b = SPLIT[half]
        far, left, right = bufs[half][1]
        out_ref[y, x, pl.ds(low, a + b), :] = (
            send[half][OWN, OWN].astype(jnp.float32)
            + far[...].astype(jnp.float32)
            + left[...].astype(jnp.float32)
            + right[...].astype(jnp.float32)
        ).astype(jnp.bfloat16)

    first = [[scatter_first(half, part) for part in range(2)] for half in range(2)]
    second = [scatter_second(half) for half in range(2)]

    def start_far(half, part):
        gather(half, part, FAR, 0, SPLIT[half][1] + SPLIT[half][2])
        first[half][part][0].start()
        first[half][part][1].start()

    def start_near(half, part):
        _, a, b = SPLIT[half]
        gather(half, part, NEXT, a, b)
        first[half][part][2].start()
        gather(half, part, PREV, 0, a)
        first[half][part][3].start()

    def gather_rest(half, part):
        _, a, b = SPLIT[half]
        gather(half, part, NEXT, 0, a)
        gather(half, part, PREV, a, b)
        gather(half, part, OWN, 0, a + b)

    def pass_on(half, part):
        for way in range(2):
            first[half][part][way].wait_recv()
            add_forward(half, part, way)
            first[half][part][4 + way].start()

    for part in range(2):
        for half in range(2):
            start_far(half, part)
    for half in range(2):
        start_near(half, 0)
    for part in range(2):
        for half in range(2):
            gather_rest(half, part)
    pre_product(z_left, 1, h1, "add")
    for half in range(2):
        pass_on(half, 0)
    for half in range(2):
        start_near(half, 1)
    for half in range(2):
        pass_on(half, 1)
    pre_product(z_right, 2, h0, "add")
    for part in range(2):
        for half in range(2):
            for n in range(2, 6):
                first[half][part][n].wait_recv()
            add_first(half, part)
            for place in parts[part]:
                if place != OWN:
                    second[half][place].start()

    def spread_copies(half):
        low, a, b = SPLIT[half]
        devices = axis(half, 1)[1]
        part = out_ref.at[y, x, pl.ds(low, a + b)]
        base = 32 * half + 15
        return [
            remote(part, part, d_send.at[base + place], d_recv.at[base + place], devices[place])
            for place in (FAR, NEXT, PREV)
        ]

    def region_copies(half, place):
        low, a, b = SPLIT[half]
        places, devices = axis(half, 0)
        q = axis(half, 1)[0][place]
        base = 32 * half + 18 + (0, 3, 7, 11)[place]

        def copy(n, column, row, count, way):
            rows = pl.ds(low + row, count)
            part = out_ref.at[q, column, rows] if half == 0 else out_ref.at[column, q, rows]
            return remote(part, part, d_send.at[base + n], d_recv.at[base + n], devices[way])

        near = (copy(0, places[OWN], 0, a + b, NEXT), copy(1, places[OWN], 0, a + b, PREV))
        if place in (FAR, OWN):
            return (*near, copy(2, places[OWN], 0, a + b, FAR))
        return (*near, copy(2, places[PREV], 0, a, NEXT), copy(3, places[NEXT], a, b, PREV))

    third = [spread_copies(half) for half in range(2)]
    fourth = [[region_copies(half, place) for place in range(4)] for half in range(2)]

    def send_region(half, place):
        for copy in fourth[half][place][: 3 if place in (FAR, OWN) else 2]:
            copy.start()

    for half in range(2):
        for copy in second[half]:
            copy.wait_recv()
        add_second(half)
        for place in (NEXT, PREV, FAR):
            third[half][place].start()
    for half in range(2):
        send_region(half, OWN)
    loads[3].wait()
    pre_product(z_far, 0, whole, "last")
    pre_copy = pltpu.make_async_copy(pre_ref, pre_out, local_sem.at[2])
    pre_copy.start()
    for place, arrived in ((NEXT, PREV), (PREV, NEXT), (FAR, FAR)):
        for half in range(2):
            third[half][arrived].wait_recv()
            send_region(half, place)
    for place in (NEXT, PREV):
        for half in range(2):
            for way in range(2):
                fourth[half][place][way].wait_recv()
                fourth[half][place][2 + way].start()
    for half in range(2):
        for place in (OWN, FAR):
            for copy in fourth[half][place]:
                copy.wait_recv()
        for place in (NEXT, PREV):
            for copy in fourth[half][place][2:]:
                copy.wait_recv()
    pre_copy.wait()

    for copy in (*z_own, s_own, *z_fwd, *s_fwd):
        copy.wait_send()
    for half in range(2):
        groups = (*first[half], second[half], third[half], *fourth[half])
        for copy in (c for group in groups for c in group):
            copy.wait_send()


def fused(u, grad_part, weights, source):
    rows_a = SPLIT[0][1] + SPLIT[0][2]
    rows_b = SPLIT[1][1] + SPLIT[1][2]
    big = [pltpu.VMEM((4, rows, LANES), jnp.bfloat16) for rows in (rows_a, rows_b) for _ in range(3)]
    small = [pltpu.VMEM((rows, LANES), jnp.bfloat16) for rows in (rows_a, rows_b) for _ in range(3)]
    vmem = pl.BlockSpec(memory_space=pltpu.VMEM)
    hbm = pl.BlockSpec(memory_space=pl.ANY)
    return pl.pallas_call(
        kernel,
        out_shape=(
            jax.ShapeDtypeStruct((TOK, HID), jnp.bfloat16),
            jax.ShapeDtypeStruct((4, 4, KEEP, LANES), jnp.bfloat16),
        ),
        in_specs=[hbm, hbm, hbm, pl.BlockSpec(memory_space=pltpu.SMEM)],
        out_specs=(hbm, vmem),
        scratch_shapes=[
            pltpu.VMEM((NBLK + GROUP, LANES), jnp.float32),
            pltpu.VMEM((3, HID, PAIR), jnp.bfloat16),
            pltpu.VMEM((4, TOK, PAIR), jnp.bfloat16),
            pltpu.VMEM((HID, TOK), jnp.bfloat16),
            pltpu.VMEM((TOK, HID), jnp.float32),
            pltpu.VMEM((TOK, HID), jnp.float32),
            pltpu.VMEM((4, 4, rows_a, LANES), jnp.bfloat16),
            pltpu.VMEM((4, 4, rows_b, LANES), jnp.bfloat16),
            pltpu.VMEM((TOK, HID), jnp.bfloat16),
            pltpu.VMEM((TOK, HID), jnp.bfloat16),
            *big,
            *small,
            pltpu.SemaphoreType.DMA((3,)),
            pltpu.SemaphoreType.DMA((4,)),
            pltpu.SemaphoreType.DMA((8,)),
            pltpu.SemaphoreType.DMA((8,)),
            pltpu.SemaphoreType.DMA((9,)),
            pltpu.SemaphoreType.DMA((9,)),
            pltpu.SemaphoreType.DMA((64,)),
            pltpu.SemaphoreType.DMA((64,)),
        ],
        compiler_params=pltpu.CompilerParams(
            collective_id=0, has_side_effects=True, vmem_limit_bytes=57 * 1024 * 1024
        ),
        cost_estimate=pl.CostEstimate(
            flops=4 * TOK * HID * WIDTH, bytes_accessed=20_000_000, transcendentals=2 * TOK * HID
        ),
    )(u, grad_part, weights, source)


FINISH = 4


def finish_kernel(pre_ref, sums_ref, pre_out, sums_out, pre_buf, sums_buf, wide_buf, in_sem, out_sem):
    slots = 16 * KEEP // FINISH
    pre_in = pltpu.make_async_copy(pre_ref, pre_buf, in_sem.at[FINISH])
    pre_back = pltpu.make_async_copy(pre_buf, pre_out, out_sem.at[FINISH])
    parts = [pl.ds(n * slots, slots) for n in range(FINISH)]
    loads = [pltpu.make_async_copy(sums_ref.at[part], sums_buf.at[part], in_sem.at[n]) for n, part in enumerate(parts)]
    stores = [pltpu.make_async_copy(wide_buf.at[part], sums_out.at[part], out_sem.at[n]) for n, part in enumerate(parts)]
    for load in loads:
        load.start()
    pre_in.start()
    for part, load, store in zip(parts, loads, stores):
        load.wait()
        wide_buf[part, :] = sums_buf[part, :].astype(jnp.float32)
        store.start()
    pre_in.wait()
    pre_back.start()
    for store in stores:
        store.wait()
    pre_back.wait()


def finish(pre_grad, sums):
    hbm = pl.BlockSpec(memory_space=pltpu.HBM)
    return pl.pallas_call(
        finish_kernel,
        out_shape=(
            jax.ShapeDtypeStruct((TOK, HID), jnp.bfloat16),
            jax.ShapeDtypeStruct((16 * KEEP, LANES), jnp.float32),
        ),
        in_specs=[hbm, hbm],
        out_specs=(hbm, hbm),
        scratch_shapes=[
            pltpu.VMEM((TOK, HID), jnp.bfloat16),
            pltpu.VMEM((16 * KEEP, LANES), jnp.bfloat16),
            pltpu.VMEM((16 * KEEP, LANES), jnp.float32),
            pltpu.SemaphoreType.DMA((FINISH + 1,)),
            pltpu.SemaphoreType.DMA((FINISH + 1,)),
        ],
    )(pre_grad, sums)


def local(
    inner_before_nonlinear,
    layer_exit_derivative,
    contract_weights,
    copy_tile_indicator,
    span_opening_tile,
    remaining_tile_flags,
):
    source = slot_sources(
        remaining_tile_flags.reshape(ROWS, LANES), copy_tile_indicator.reshape(ROWS, LANES), span_opening_tile
    )
    pre_grad, sums = fused(inner_before_nonlinear, layer_exit_derivative, contract_weights, source)
    pre_grad, sums = finish(pre_grad, sums.reshape(16 * KEEP, LANES))
    return (pre_grad, sums[None])


def solution(mesh):
    in_specs = (
        P("dp", "mp"),
        P("dp", "mp"),
        P("mp", None),
        P("dp", "mp", None),
        P(),
        P("mp", None),
    )
    out_specs = (P("dp", "mp"), P("mp", None, None))
    return jax.shard_map(local, mesh=mesh, in_specs=in_specs, out_specs=out_specs, check_vma=False)
```

time: 101 us -> 79.4 us (0.79); the launches traced: 99.3 us -> 79.1 us
  other arithmetic: 11.9 us -> 0 us
  Pallas kernels: 82.7 us -> 78.5 us
  matrix products: 2.51 us -> 0 us
  local copies, waits for them, and re-layouts: 1.48 us -> 0 us
    pallas_call x1, Pallas kernels: 82.7 us -> 71 us  [fused(): pl.pallas_call(kernel, out_shape=(jax.ShapeDtypeStruct((TOK, HID), jnp.bf...]
    pallas_call x0 -> x2, Pallas kernels: none -> 7.47 us  [the longest x1 4.19 us: slot_sources(): pl.pallas_call(index_kernel, out_shape=jax.ShapeDtypeStruct((1, 16 * SLOT...]
    convert_element_type x5 -> x0, other arithmetic: 6.42 us -> none  [the longest x1 3.45 us: local(): return (pre_grad, sums.reshape(1, 16 * KEEP, LANES).astype(jnp.float32))]
    reduce_sum x5 -> x0, other arithmetic: 4.62 us -> none  [the longest x1 1.99 us: slot_sources(): rest = target - jnp.sum(jnp.where(passed, totals[None, :], 0), axis=1)]
    dot_general x2 -> x0, matrix products: 2.51 us -> none  [the longest x1 2.34 us: slot_sources(): picked = jnp.dot(pick, table, preferred_element_type=jnp.float32)]
    unnamed x3 -> x0, local copies, waits for them, and re-layouts: 1.06 us -> none
where the time goes in v2:
time: 79.4 us; the launch traced here: 79.1 us
  Pallas kernels  78.5 us (99%)
    pallas_call x1, Pallas kernels, fused(): pl.pallas_call(kernel, out_shape=(jax.ShapeDtypeStruct((TOK, HID), jnp.bf...  71 us
    pallas_call x1, Pallas kernels, slot_sources(): pl.pallas_call(index_kernel, out_shape=jax.ShapeDtypeStruct((1, 16 * SLOT...  4.19 us
    pallas_call x1, Pallas kernels, finish(): pl.pallas_call(finish_kernel, out_shape=(jax.ShapeDtypeStruct((TOK, HID),...  3.28 us

profile of v2, /device:TPU:0, one launch (start us, length us, event | category | flops | bytes accessed | tf_op | source)
XLA Modules:
  0.0 79.1 jit_solution(2828934354762002824)
XLA Ops:
  0.6 4.2 %shard_map.77.src_ref = s32[1,8192]{1,0:T(1,128)} custom-call(s32[400,128]{1,0:T(8,128)} %bitcast.5, s32[400,128]{1,0:T(8,128)} %bitcast.6, s32[17]{0:T(128)} %start_ref.1), custom_call_target="tpu_custom_call" | custom-call | tf_op jit(solution)/shard_map/pallas_call | solution.py:97
  4.8 71.0 %shard_map.78 = (bf16[512,1280]{1,0:T(8,128)(2,1)}, bf16[4,4,400,128]{3,2,1,0:T(8,128)(2,1)}) custom-call(bf16[512,1280]{1,0:T(8,128)(2,1)} %u_ref.1, bf16[512,640]{1,0:T(8,128)(2,1)} %g_ref.1, bf16[1280,5120]{1,0:T(8,128)(2,1)} %w_ref.1, s32[1,8192]{1,0:T(1,128)} %shard_map.77.src_ref), custom_call_target="tpu_custom_call" | custom-call | flops 13421772800 | bytes 20000000 | tf_op jit(solution)/shard_map/pallas_call | solution.py:528
  75.8 3.3 %shard_map.79 = (bf16[512,1280]{1,0:T(8,128)(2,1)}, f32[6400,128]{1,0:T(8,128)}) custom-call(bf16[512,1280]{1,0:T(8,128)(2,1)} %get-tuple-element.6.pre_ref, bf16[6400,128]{1,0:T(8,128)(2,1)} %bitcast.4), custom_call_target="tpu_custom_call" | custom-call | tf_op jit(solution)/shard_map/pallas_call | solution.py:593

commit v3 on v2

--- a/solution.py
+++ b/solution.py
@@ -27,16 +27,14 @@
 ROWS_PAD = 448
 WINDOW = 48
 SLOTS = 512
-CUT = 384
+CUT = 256
 SPLIT = ((0, 112, 96), (208, 96, 96))
 
 
-def index_kernel(flag_ref, copied_ref, start_ref, src_ref, flags, copied, within, upto, before, opening):
+def index_kernel(flag_ref, copied_ref, start_ref, src_ref, flags, within, upto, before, opening):
     flags[pl.ds(0, ROWS), :] = flag_ref[...]
-    copied[pl.ds(0, ROWS), :] = copied_ref[...].astype(jnp.float32)
     pad = pl.ds(ROWS, ROWS_PAD - ROWS)
     flags[pad, :] = jnp.zeros((ROWS_PAD - ROWS, LANES), jnp.int32)
-    copied[pad, :] = jnp.zeros((ROWS_PAD - ROWS, LANES), jnp.float32)
 
     def iota(shape, dim):
         return lax.broadcasted_iota(jnp.int32, shape, dim)
@@ -44,7 +42,9 @@
     square = (LANES, LANES)
     flag_bf = flags[...].astype(jnp.float32).astype(jnp.bfloat16)
     tri = jnp.where(iota(square, 0) <= iota(square, 1), 1.0, 0.0).astype(jnp.bfloat16)
-    within[...] = jnp.dot(flag_bf, tri, preferred_element_type=jnp.float32)
+    within[...] = jnp.dot(flag_bf, tri, preferred_element_type=jnp.float32) - 64.0
+    both = (flag_ref[...] * copied_ref[...]).astype(jnp.float32)
+    within[pl.ds(0, ROWS), :] = within[pl.ds(0, ROWS), :] + 0.5 * both
     totals = jnp.dot(flag_bf, jnp.ones(square, jnp.bfloat16), preferred_element_type=jnp.float32)
     tall = (ROWS_PAD, ROWS_PAD)
     tri = jnp.where(iota(tall, 0) >= iota(tall, 1), 1.0, 0.0).astype(jnp.bfloat16)
@@ -71,16 +71,12 @@
         last = jnp.max(jnp.where(passed, ends, wide(before[pl.ds(row0, 1), :])), axis=0, keepdims=True)
         pick = jnp.where(iota((WINDOW, SLOTS), 0).astype(jnp.float32) == count, 1.0, 0.0).astype(jnp.bfloat16)
 
-        def lookup(table):
-            return lax.dot_general(
-                table.astype(jnp.bfloat16), pick, (((0,), (0,)), ((), ())), preferred_element_type=jnp.float32
-            )
-
-        at = jnp.sum(jnp.where(lookup(within[rows, :]) <= target - last, 1.0, 0.0), axis=0, keepdims=True)
-        here = iota((LANES, SLOTS), 0).astype(jnp.float32) == at
-        kept = jnp.sum(
-            jnp.where(here, lookup(copied[rows, :]), 0.0), axis=0, keepdims=True
+        found = lax.dot_general(
+            within[rows, :].astype(jnp.bfloat16), pick, (((0,), (0,)), ((), ())), preferred_element_type=jnp.float32
         )
+        rest = target - last - 64.0
+        at = jnp.sum(jnp.where(found < rest + 0.75, 1.0, 0.0), axis=0, keepdims=True)
+        kept = jnp.sum(jnp.where(found == rest + 1.5, 1.0, 0.0), axis=0, keepdims=True)
         block = (count + row0.astype(jnp.float32)) * LANES + at
         hid = jnp.floor((block + 0.5) * (1.0 / COLS))
         source = (block - hid * COLS) * HID + hid
@@ -104,7 +100,6 @@
             table,
             table,
             table,
-            table,
             pltpu.VMEM((24, LANES), jnp.float32),
         ],
     )(flags, copied, starts)
@@ -112,10 +107,10 @@
 
 def kernel(
     u_ref, g_ref, w_ref, src_ref,
-    pre_out, out_ref,
-    wg, wbuf, grad, act_t, slope, acc, send_a, send_b, u_buf, pre_ref,
+    pre_out, sums_out,
+    wg, wbuf, grad, act_t, slope, acc, send_a, send_b, out_ref, u_buf, pre_ref,
     f1a, l1a, r1a, f1b, l1b, r1b, f2a, l2a, r2a, f2b, l2b, r2b,
-    local_sem, w_sem, z_send, z_recv, s_send, s_recv, d_send, d_recv,
+    local_sem, out_sem, w_sem, z_send, z_recv, s_send, s_recv, d_send, d_recv,
 ):
     dp = lax.axis_index("dp")
     mp = lax.axis_index("mp")
@@ -315,44 +310,36 @@
 
     def gather(half, part, place, row, count):
         low = SPLIT[half][0]
-        groups = count // GROUP
         one = axis(half, 0)[0][place]
+        regions = []
         for second in parts[part]:
             two = axis(half, 1)[0][second]
-            region = two * 4 + one if half == 0 else one * 4 + two
-
-            def body(n, carry):
-                at = pl.multiple_of(row + n * GROUP, GROUP)
-                first = region * SLOTS + low + at
-                taken = [wg[pl.ds(src_ref[0, first + s], 1), :] for s in range(GROUP)]
+            regions.append((second, (two * 4 + one if half == 0 else one * 4 + two) * SLOTS + low))
+
+        def body(n, carry):
+            at = pl.multiple_of(row + n * GROUP, GROUP)
+            for second, first in regions:
+                taken = [wg[pl.ds(src_ref[0, first + at + s], 1), :] for s in range(GROUP)]
                 send[half][second, place, pl.ds(at, GROUP), :] = (
                     jnp.concatenate(taken, axis=0) * scale
                 ).astype(jnp.bfloat16)
-                return carry
-
-            lax.fori_loop(0, groups, body, 0)
+            return carry
+
+        lax.fori_loop(0, count // GROUP, body, 0)
 
     def scatter_first(half, part):
-        _, a, b = SPLIT[half]
-        fwd, left, right = bufs[half][0]
         devices = axis(half, 0)[1]
         lead = pl.ds(2 * part, 2)
-        base = 32 * half + 6 * part
-
-        def copy(n, place, row, count, dst, way):
+        base = 32 * half + 3 * part
+
+        def copy(place, dst):
             return remote(
-                send[half].at[lead, place, pl.ds(row, count)], dst.at[lead, pl.ds(row, count)],
-                d_send.at[base + n], d_recv.at[base + n], devices[way],
+                send[half].at[lead, place], dst.at[lead], d_send.at[base + place], d_recv.at[base + place],
+                devices[place],
             )
 
-        return (
-            copy(0, FAR, 0, a, fwd, NEXT),
-            copy(1, FAR, a, b, fwd, PREV),
-            copy(2, NEXT, a, b, left, NEXT),
-            copy(3, PREV, 0, a, right, PREV),
-            copy(4, NEXT, 0, a, left, NEXT),
-            copy(5, PREV, a, b, right, PREV),
-        )
+        far, left, right = bufs[half][0]
+        return (copy(FAR, far), copy(NEXT, left), copy(PREV, right))
 
     def scatter_second(half):
         devices = axis(half, 1)[1]
@@ -366,21 +353,12 @@
 
         return (copy(0, FAR, far), copy(1, NEXT, left), copy(2, PREV, right))
 
-    def add_forward(half, part, way):
-        _, a, b = SPLIT[half]
-        fwd = bufs[half][0][0]
-        row, count, place = ((0, a, NEXT), (a, b, PREV))[way]
-        rows = pl.ds(row, count)
-        for second in parts[part]:
-            send[half][second, place, rows, :] = (
-                send[half][second, place, rows, :].astype(jnp.float32) + fwd[second, rows, :].astype(jnp.float32)
-            ).astype(jnp.bfloat16)
-
     def add_first(half, part):
-        _, left, right = bufs[half][0]
+        far, left, right = bufs[half][0]
         for second in parts[part]:
             send[half][second, OWN] = (
                 send[half][second, OWN].astype(jnp.float32)
+                + far[second].astype(jnp.float32)
                 + left[second].astype(jnp.float32)
                 + right[second].astype(jnp.float32)
             ).astype(jnp.bfloat16)
@@ -398,54 +376,26 @@
     first = [[scatter_first(half, part) for part in range(2)] for half in range(2)]
     second = [scatter_second(half) for half in range(2)]
 
-    def start_far(half, part):
-        gather(half, part, FAR, 0, SPLIT[half][1] + SPLIT[half][2])
-        first[half][part][0].start()
-        first[half][part][1].start()
-
-    def start_near(half, part):
-        _, a, b = SPLIT[half]
-        gather(half, part, NEXT, a, b)
-        first[half][part][2].start()
-        gather(half, part, PREV, 0, a)
-        first[half][part][3].start()
-
-    def gather_rest(half, part):
-        _, a, b = SPLIT[half]
-        gather(half, part, NEXT, 0, a)
-        gather(half, part, PREV, a, b)
-        gather(half, part, OWN, 0, a + b)
-
-    def pass_on(half, part):
-        for way in range(2):
-            first[half][part][way].wait_recv()
-            add_forward(half, part, way)
-            first[half][part][4 + way].start()
-
+    for part in range(2):
+        for place in (FAR, NEXT, PREV):
+            for half in range(2):
+                gather(half, part, place, 0, SPLIT[half][1] + SPLIT[half][2])
+                first[half][part][place].start()
     for part in range(2):
         for half in range(2):
-            start_far(half, part)
-    for half in range(2):
-        start_near(half, 0)
+            gather(half, part, OWN, 0, SPLIT[half][1] + SPLIT[half][2])
     for part in range(2):
         for half in range(2):
-            gather_rest(half, part)
-    pre_product(z_left, 1, h1, "add")
-    for half in range(2):
-        pass_on(half, 0)
-    for half in range(2):
-        start_near(half, 1)
-    for half in range(2):
-        pass_on(half, 1)
-    pre_product(z_right, 2, h0, "add")
-    for part in range(2):
-        for half in range(2):
-            for n in range(2, 6):
-                first[half][part][n].wait_recv()
+            for copy in first[half][part]:
+                copy.wait_recv()
             add_first(half, part)
             for place in parts[part]:
                 if place != OWN:
                     second[half][place].start()
+        if part == 0:
+            pre_product(z_left, 1, h1, "add")
+        else:
+            pre_product(z_right, 2, h0, "add")
 
     def spread_copies(half):
         low, a, b = SPLIT[half]
@@ -461,23 +411,20 @@
         low, a, b = SPLIT[half]
         places, devices = axis(half, 0)
         q = axis(half, 1)[0][place]
-        base = 32 * half + 18 + (0, 3, 7, 11)[place]
+        base = 32 * half + 18 + 3 * place
 
         def copy(n, column, row, count, way):
             rows = pl.ds(low + row, count)
             part = out_ref.at[q, column, rows] if half == 0 else out_ref.at[column, q, rows]
             return remote(part, part, d_send.at[base + n], d_recv.at[base + n], devices[way])
 
-        near = (copy(0, places[OWN], 0, a + b, NEXT), copy(1, places[OWN], 0, a + b, PREV))
-        if place in (FAR, OWN):
-            return (*near, copy(2, places[OWN], 0, a + b, FAR))
-        return (*near, copy(2, places[PREV], 0, a, NEXT), copy(3, places[NEXT], a, b, PREV))
+        return tuple(copy(n, places[OWN], 0, a + b, way) for n, way in enumerate((NEXT, PREV, FAR)))
 
     third = [spread_copies(half) for half in range(2)]
     fourth = [[region_copies(half, place) for place in range(4)] for half in range(2)]
 
     def send_region(half, place):
-        for copy in fourth[half][place][: 3 if place in (FAR, OWN) else 2]:
+        for copy in fourth[half][place]:
             copy.start()
 
     for half in range(2):
@@ -496,18 +443,18 @@
         for half in range(2):
             third[half][arrived].wait_recv()
             send_region(half, place)
-    for place in (NEXT, PREV):
+    stores = []
+    for place in (OWN, NEXT, PREV, FAR):
         for half in range(2):
-            for way in range(2):
-                fourth[half][place][way].wait_recv()
-                fourth[half][place][2 + way].start()
-    for half in range(2):
-        for place in (OWN, FAR):
+            low, a, b = SPLIT[half]
             for copy in fourth[half][place]:
                 copy.wait_recv()
-        for place in (NEXT, PREV):
-            for copy in fourth[half][place][2:]:
-                copy.wait_recv()
+            q, rows = axis(half, 1)[0][place], pl.ds(low, a + b)
+            at = (q, slice(None), rows) if half == 0 else (slice(None), q, rows)
+            stores.append(pltpu.make_async_copy(out_ref.at[at], sums_out.at[at], out_sem.at[4 * half + place]))
+            stores[-1].start()
+    for store in stores:
+        store.wait()
     pre_copy.wait()
 
     for copy in (*z_own, s_own, *z_fwd, *s_fwd):
@@ -532,7 +479,7 @@
             jax.ShapeDtypeStruct((4, 4, KEEP, LANES), jnp.bfloat16),
         ),
         in_specs=[hbm, hbm, hbm, pl.BlockSpec(memory_space=pltpu.SMEM)],
-        out_specs=(hbm, vmem),
+        out_specs=(hbm, hbm),
         scratch_shapes=[
             pltpu.VMEM((NBLK + GROUP, LANES), jnp.float32),
             pltpu.VMEM((3, HID, PAIR), jnp.bfloat16),
@@ -542,11 +489,13 @@
             pltpu.VMEM((TOK, HID), jnp.float32),
             pltpu.VMEM((4, 4, rows_a, LANES), jnp.bfloat16),
             pltpu.VMEM((4, 4, rows_b, LANES), jnp.bfloat16),
+            pltpu.VMEM((4, 4, KEEP, LANES), jnp.bfloat16),
             pltpu.VMEM((TOK, HID), jnp.bfloat16),
             pltpu.VMEM((TOK, HID), jnp.bfloat16),
             *big,
             *small,
             pltpu.SemaphoreType.DMA((3,)),
+            pltpu.SemaphoreType.DMA((8,)),
             pltpu.SemaphoreType.DMA((4,)),
             pltpu.SemaphoreType.DMA((8,)),
             pltpu.SemaphoreType.DMA((8,)),
@@ -574,15 +523,15 @@
     parts = [pl.ds(n * slots, slots) for n in range(FINISH)]
     loads = [pltpu.make_async_copy(sums_ref.at[part], sums_buf.at[part], in_sem.at[n]) for n, part in enumerate(parts)]
     stores = [pltpu.make_async_copy(wide_buf.at[part], sums_out.at[part], out_sem.at[n]) for n, part in enumerate(parts)]
+    pre_in.start()
     for load in loads:
         load.start()
-    pre_in.start()
+    pre_in.wait()
+    pre_back.start()
     for part, load, store in zip(parts, loads, stores):
         load.wait()
         wide_buf[part, :] = sums_buf[part, :].astype(jnp.float32)
         store.start()
-    pre_in.wait()
-    pre_back.start()
     for store in stores:
         store.wait()
     pre_back.wait()

time: 79.4 us -> 75 us (0.945)
  Pallas kernels: 78.5 us -> 74.1 us
    pallas_call x1, Pallas kernels: 71 us -> 66.6 us  [fused(): pl.pallas_call(kernel, out_shape=(jax.ShapeDtypeStruct((TOK, HID), jnp.bf...]
where the time goes in v3:
time: 75 us; the launch traced here: 74.7 us
  Pallas kernels  74.1 us (99%)
    pallas_call x1, Pallas kernels, fused(): pl.pallas_call(kernel, out_shape=(jax.ShapeDtypeStruct((TOK, HID), jnp.bf...  66.6 us
    pallas_call x1, Pallas kernels, slot_sources(): pl.pallas_call(index_kernel, out_shape=jax.ShapeDtypeStruct((1, 16 * SLOT...  3.96 us
    pallas_call x1, Pallas kernels, finish(): pl.pallas_call(finish_kernel, out_shape=(jax.ShapeDtypeStruct((TOK, HID),...  3.54 us

profile of v3, /device:TPU:0, one launch (start us, length us, event | category | flops | bytes accessed | tf_op | source)
XLA Modules:
  0.0 74.7 jit_solution(6594975656496033353)
XLA Ops:
  0.6 4.0 %shard_map.77.src_ref = s32[1,8192]{1,0:T(1,128)} custom-call(s32[400,128]{1,0:T(8,128)} %bitcast.5, s32[400,128]{1,0:T(8,128)} %bitcast.6, s32[17]{0:T(128)} %start_ref.1), custom_call_target="tpu_custom_call" | custom-call | tf_op jit(solution)/shard_map/pallas_call | solution.py:93
  4.6 66.6 %shard_map.78 = (bf16[512,1280]{1,0:T(8,128)(2,1)}, bf16[4,4,400,128]{3,2,1,0:T(8,128)(2,1)}) custom-call(bf16[512,1280]{1,0:T(8,128)(2,1)} %u_ref.1, bf16[512,640]{1,0:T(8,128)(2,1)} %g_ref.1, bf16[1280,5120]{1,0:T(8,128)(2,1)} %w_ref.1, s32[1,8192]{1,0:T(1,128)} %shard_map.77.src_ref), custom_call_target="tpu_custom_call" | custom-call | flops 13421772800 | bytes 20000000 | tf_op jit(solution)/shard_map/pallas_call | solution.py:475
  71.2 3.5 %shard_map.79 = (bf16[512,1280]{1,0:T(8,128)(2,1)}, f32[6400,128]{1,0:T(8,128)}) custom-call(bf16[512,1280]{1,0:T(8,128)(2,1)} %get-tuple-element.6.pre_ref, bf16[6400,128]{1,0:T(8,128)(2,1)} %bitcast.4), custom_call_target="tpu_custom_call" | custom-call | tf_op jit(solution)/shard_map/pallas_call | solution.py:542

commit v4 on v3

--- a/solution.py
+++ b/solution.py
@@ -295,7 +295,7 @@
     scale = 1.0 / math.sqrt(TOK * 16)
     FAR, NEXT, PREV, OWN = range(4)
     SHIFT = (2, 1, -1, 0)
-    parts = ((FAR, NEXT), (PREV, OWN))
+    parts = ((FAR,), (NEXT, PREV), (OWN,))
     send = (send_a, send_b)
     bufs = (
         ((f1a, l1a, r1a), (f2a, l2a, r2a)),
@@ -329,7 +329,7 @@
 
     def scatter_first(half, part):
         devices = axis(half, 0)[1]
-        lead = pl.ds(2 * part, 2)
+        lead = pl.ds(parts[part][0], len(parts[part]))
         base = 32 * half + 3 * part
 
         def copy(place, dst):
@@ -373,18 +373,18 @@
             + right[...].astype(jnp.float32)
         ).astype(jnp.bfloat16)
 
-    first = [[scatter_first(half, part) for part in range(2)] for half in range(2)]
+    first = [[scatter_first(half, part) for part in range(3)] for half in range(2)]
     second = [scatter_second(half) for half in range(2)]
 
-    for part in range(2):
+    for part in range(3):
         for place in (FAR, NEXT, PREV):
             for half in range(2):
                 gather(half, part, place, 0, SPLIT[half][1] + SPLIT[half][2])
                 first[half][part][place].start()
-    for part in range(2):
+    for part in range(3):
         for half in range(2):
             gather(half, part, OWN, 0, SPLIT[half][1] + SPLIT[half][2])
-    for part in range(2):
+    for part in range(3):
         for half in range(2):
             for copy in first[half][part]:
                 copy.wait_recv()
@@ -394,7 +394,7 @@
                     second[half][place].start()
         if part == 0:
             pre_product(z_left, 1, h1, "add")
-        else:
+        elif part == 1:
             pre_product(z_right, 2, h0, "add")
 
     def spread_copies(half):
@@ -523,15 +523,15 @@
     parts = [pl.ds(n * slots, slots) for n in range(FINISH)]
     loads = [pltpu.make_async_copy(sums_ref.at[part], sums_buf.at[part], in_sem.at[n]) for n, part in enumerate(parts)]
     stores = [pltpu.make_async_copy(wide_buf.at[part], sums_out.at[part], out_sem.at[n]) for n, part in enumerate(parts)]
-    pre_in.start()
     for load in loads:
         load.start()
-    pre_in.wait()
-    pre_back.start()
+    pre_in.start()
     for part, load, store in zip(parts, loads, stores):
         load.wait()
         wide_buf[part, :] = sums_buf[part, :].astype(jnp.float32)
         store.start()
+    pre_in.wait()
+    pre_back.start()
     for store in stores:
         store.wait()
     pre_back.wait()

time: 75 us -> 73.3 us (0.977)
  Pallas kernels: 74.1 us -> 72.4 us
    pallas_call x1, Pallas kernels: 66.6 us -> 65.2 us  [fused(): pl.pallas_call(kernel, out_shape=(jax.ShapeDtypeStruct((TOK, HID), jnp.bf...]
where the time goes in v4:
time: 73.3 us; the launch traced here: 73 us
  Pallas kernels  72.4 us (99%)
    pallas_call x1, Pallas kernels, fused(): pl.pallas_call(kernel, out_shape=(jax.ShapeDtypeStruct((TOK, HID), jnp.bf...  65.2 us
    pallas_call x1, Pallas kernels, slot_sources(): pl.pallas_call(index_kernel, out_shape=jax.ShapeDtypeStruct((1, 16 * SLOT...  3.96 us
    pallas_call x1, Pallas kernels, finish(): pl.pallas_call(finish_kernel, out_shape=(jax.ShapeDtypeStruct((TOK, HID),...  3.28 us

profile of v4, /device:TPU:0, one launch (start us, length us, event | category | flops | bytes accessed | tf_op | source)
XLA Modules:
  0.0 73.0 jit_solution(2975126054677767050)
XLA Ops:
  0.6 4.0 %shard_map.77.src_ref = s32[1,8192]{1,0:T(1,128)} custom-call(s32[400,128]{1,0:T(8,128)} %bitcast.5, s32[400,128]{1,0:T(8,128)} %bitcast.6, s32[17]{0:T(128)} %start_ref.1), custom_call_target="tpu_custom_call" | custom-call | tf_op jit(solution)/shard_map/pallas_call | solution.py:93
  4.6 65.2 %shard_map.78 = (bf16[512,1280]{1,0:T(8,128)(2,1)}, bf16[4,4,400,128]{3,2,1,0:T(8,128)(2,1)}) custom-call(bf16[512,1280]{1,0:T(8,128)(2,1)} %u_ref.1, bf16[512,640]{1,0:T(8,128)(2,1)} %g_ref.1, bf16[1280,5120]{1,0:T(8,128)(2,1)} %w_ref.1, s32[1,8192]{1,0:T(1,128)} %shard_map.77.src_ref), custom_call_target="tpu_custom_call" | custom-call | flops 13421772800 | bytes 20000000 | tf_op jit(solution)/shard_map/pallas_call | solution.py:475
  69.8 3.3 %shard_map.79 = (bf16[512,1280]{1,0:T(8,128)(2,1)}, f32[6400,128]{1,0:T(8,128)}) custom-call(bf16[512,1280]{1,0:T(8,128)(2,1)} %get-tuple-element.6.pre_ref, bf16[6400,128]{1,0:T(8,128)(2,1)} %bitcast.4), custom_call_target="tpu_custom_call" | custom-call | tf_op jit(solution)/shard_map/pallas_call | solution.py:542

commit v5 on v4

--- a/solution.py
+++ b/solution.py
@@ -27,7 +27,7 @@
 ROWS_PAD = 448
 WINDOW = 48
 SLOTS = 512
-CUT = 256
+CUT = 128
 SPLIT = ((0, 112, 96), (208, 96, 96))
 
 
@@ -228,7 +228,7 @@
 
         lax.fori_loop(0, PAIR // 256, body, 0)
 
-    def pre_product(zp, slot, rows, mode):
+    def pre_product(zp, slot, rows, mode, low=0, high=HID // 256):
         def body(n, carry):
             hid = pl.ds(pl.multiple_of(n * 256, LANES), 256)
             product = lax.dot_general(
@@ -243,7 +243,7 @@
                 pre_ref[rows, hid] = ((acc[rows, hid] + product) * slope[rows, hid]).astype(jnp.bfloat16)
             return carry
 
-        lax.fori_loop(0, HID // 256, body, 0)
+        lax.fori_loop(low, high, body, 0)
 
     whole = pl.ds(0, TOK)
     own_copy.wait()
@@ -436,13 +436,14 @@
     for half in range(2):
         send_region(half, OWN)
     loads[3].wait()
-    pre_product(z_far, 0, whole, "last")
-    pre_copy = pltpu.make_async_copy(pre_ref, pre_out, local_sem.at[2])
-    pre_copy.start()
+    pre_product(z_far, 0, whole, "last", 0, 3)
     for place, arrived in ((NEXT, PREV), (PREV, NEXT), (FAR, FAR)):
         for half in range(2):
             third[half][arrived].wait_recv()
             send_region(half, place)
+    pre_product(z_far, 0, whole, "last", 3)
+    pre_copy = pltpu.make_async_copy(pre_ref, pre_out, local_sem.at[2])
+    pre_copy.start()
     stores = []
     for place in (OWN, NEXT, PREV, FAR):
         for half in range(2):

time: 73.3 us -> 73.2 us (level)
  no operation moved by 1% of the time
where the time goes in v5:
time: 73.2 us; the launch traced here: 72.9 us
  Pallas kernels  72.2 us (99%)
    pallas_call x1, Pallas kernels, fused(): pl.pallas_call(kernel, out_shape=(jax.ShapeDtypeStruct((TOK, HID), jnp.bf...  65 us
    pallas_call x1, Pallas kernels, slot_sources(): pl.pallas_call(index_kernel, out_shape=jax.ShapeDtypeStruct((1, 16 * SLOT...  3.96 us
    pallas_call x1, Pallas kernels, finish(): pl.pallas_call(finish_kernel, out_shape=(jax.ShapeDtypeStruct((TOK, HID),...  3.28 us

profile of v5, /device:TPU:0, one launch (start us, length us, event | category | flops | bytes accessed | tf_op | source)
XLA Modules:
  0.0 72.9 jit_solution(11401634676566023924)
XLA Ops:
  0.6 4.0 %shard_map.77.src_ref = s32[1,8192]{1,0:T(1,128)} custom-call(s32[400,128]{1,0:T(8,128)} %bitcast.5, s32[400,128]{1,0:T(8,128)} %bitcast.6, s32[17]{0:T(128)} %start_ref.1), custom_call_target="tpu_custom_call" | custom-call | tf_op jit(solution)/shard_map/pallas_call | solution.py:93
  4.6 65.0 %shard_map.78 = (bf16[512,1280]{1,0:T(8,128)(2,1)}, bf16[4,4,400,128]{3,2,1,0:T(8,128)(2,1)}) custom-call(bf16[512,1280]{1,0:T(8,128)(2,1)} %u_ref.1, bf16[512,640]{1,0:T(8,128)(2,1)} %g_ref.1, bf16[1280,5120]{1,0:T(8,128)(2,1)} %w_ref.1, s32[1,8192]{1,0:T(1,128)} %shard_map.77.src_ref), custom_call_target="tpu_custom_call" | custom-call | flops 13421772800 | bytes 20000000 | tf_op jit(solution)/shard_map/pallas_call | solution.py:476
  69.6 3.3 %shard_map.79 = (bf16[512,1280]{1,0:T(8,128)(2,1)}, f32[6400,128]{1,0:T(8,128)}) custom-call(bf16[512,1280]{1,0:T(8,128)(2,1)} %get-tuple-element.6.pre_ref, bf16[6400,128]{1,0:T(8,128)(2,1)} %bitcast.4), custom_call_target="tpu_custom_call" | custom-call | tf_op jit(solution)/shard_map/pallas_call | solution.py:543
